TPU v7x, 512 devices: a whole 4x4x16 slice. The times are simulated.
512 devices in a mesh: atm: 32 (over z_lo, y), ocn: 16 (over x, z_hi, core).
Axes of the slice: x: 4, y: 4, z: 16 (z_hi: 2, z_lo: 8; z = z_hi * 8 + z_lo), core: 2. Of those that a mesh axis runs over, the one named last changes fastest.
Arguments:
- atm_fields: float32 [16384, 16, 128], P(('atm', 'ocn')), may hold values from -6 to 6
- coupler_map: int32 [16, 1024], P('ocn'), may hold values from 0 to 1023, as said below
- remap_pattern: int32 [16384], P(('atm', 'ocn')), may hold values from 0 to 31, as said below
- remap_weights: float32 [16384, 128, 256], P(('atm', 'ocn')), may hold values from -0.375 to 0.375
- bulk_coeffs: float32 [4, 16], replicated, may hold values from -1.5 to 1.5
- ocean_state: float32 [4, 1024, 2048], P(None, 'atm', 'ocn'), may hold values from -6 to 6
- land_mask: int32 [1024, 2048], P('atm', 'ocn'), may hold values 0 or 1
Outputs:
- ocean_next: float32 [4, 1024, 2048], P(None, 'atm', 'ocn')
- atm_return: float32 [16384, 4, 128], P(('atm', 'ocn'))
Inputs may be any that keep to these rules, and one draw needn't show every extreme that they name: `coupler_map`: each row is a permutation; of the 32 slots of one coupler device, exactly 1 come from each device of the same column. `remap_pattern`: the 32 entries of one device are a permutation of its local blocks.
All inputs are finite; a program needn't handle non-finite values. No bound on the sum of `land_mask` on one device may be relied on, other than what follows from the above.
Results may differ from a plain program's by a relative error of at most 0.00007.
Values sent between devices are 32-bit elements; how exact they have to be, the bound alone decides.
A program may use at most 64 MiB of HBM per device.

v0:
```python
import jax
import jax.numpy as jnp
from jax import lax
from jax.sharding import PartitionSpec as P

BS = 128
NNZ = 2
SUBSTEPS = 2


def padded_2(array, sides, width):
    for axis, dim in sides:
        devices, length = (lax.axis_size(axis), array.shape[dim])
        up = [(i, (i + 1) % devices) for i in range(devices - 1)]
        down = [(j, i) for i, j in up]
        last = lax.slice_in_dim(array, length - width, length, axis=dim)
        leading = lax.slice_in_dim(array, 0, width, axis=dim)
        before = lax.ppermute(last, axis, up)
        after = lax.ppermute(leading, axis, down)
        array = jnp.concatenate([before, array, after], axis=dim)
    return array


def advance(ocean_now, padded, forcing, wet_cells):
    laplace = (
        padded[:, 2:, 1:-1]
        + padded[:, :-2, 1:-1]
        + padded[:, 1:-1, 2:]
        + padded[:, 1:-1, :-2]
        - 4.0 * ocean_now
    )
    zero_field = jnp.zeros_like(ocean_now[0])
    rotation = jnp.stack([ocean_now[1], -ocean_now[0], zero_field, zero_field])
    kappa = jnp.array([0.8, 0.8, 0.5, 0.5], jnp.float32)[:, None, None]
    tendency = kappa * laplace + 0.5 * rotation - 0.1 * ocean_now + forcing
    return wet_cells * (ocean_now + 0.25 * tendency)


def body(
    atm_fields, coupler_map, remap_pattern, remap_weights, bulk_coeffs, ocean_state, land_mask
):
    highest = lax.Precision.HIGHEST
    atm_count = lax.axis_size("atm")
    ocn_count = lax.axis_size("ocn")
    blocks = atm_fields.shape[0]
    per_peer = blocks // atm_count
    position = lax.axis_index("atm")
    slot_table = coupler_map[0]
    inverse = (
        jnp.zeros((atm_count * blocks,), jnp.int32)
        .at[slot_table]
        .set(jnp.arange(atm_count * blocks, dtype=jnp.int32))
    )
    targets = lax.dynamic_slice_in_dim(inverse, position * blocks, blocks)
    send_order = jnp.argsort(targets)
    sources = lax.dynamic_slice_in_dim(slot_table, position * blocks, blocks) // blocks
    onehot = (sources[:, None] == jnp.arange(atm_count, dtype=jnp.int32)[None, :]).astype(jnp.int32)
    peer_rank = jnp.sum(onehot * (jnp.cumsum(onehot, axis=0) - onehot), axis=1)
    receive_index = sources * per_peer + peer_rank
    weights = remap_weights.reshape(ocn_count, NNZ, BS, remap_weights.shape[2])
    pattern = remap_pattern.reshape(ocn_count, NNZ)
    outgoing_blocks = atm_fields[send_order]
    arrived_blocks = lax.all_to_all(outgoing_blocks, "atm", split_axis=0, concat_axis=0, tiled=True)
    gathered = arrived_blocks[receive_index][pattern]
    forcing_rows = jnp.einsum("dkfb,dkbq->fdq", gathered, weights, precision=highest)
    arrived = lax.all_to_all(forcing_rows, "ocn", split_axis=1, concat_axis=1, tiled=True)
    tile_rows = arrived.reshape(arrived.shape[0], land_mask.shape[0], land_mask.shape[1])
    forcing = jnp.einsum("sf,fxy->sxy", bulk_coeffs, tile_rows, precision=highest)
    wet_cells = land_mask.astype(jnp.float32)
    ocean_now = ocean_state
    for substep in range(SUBSTEPS):
        padded = padded_2(ocean_now, (("atm", 1), ("ocn", 2)), 1)
        ocean_now = advance(ocean_now, padded, forcing, wet_cells)
    outgoing = ocean_now.reshape(ocean_now.shape[0], ocn_count, -1)
    back_rows = lax.all_to_all(outgoing, "ocn", split_axis=1, concat_axis=1, tiled=True)
    back_terms = jnp.einsum("cdq,dkbq->dkcb", back_rows, weights, precision=highest)
    back_terms = back_terms.reshape(blocks, ocean_now.shape[0], BS)
    returned = jnp.zeros_like(back_terms).at[remap_pattern].add(back_terms)
    return (ocean_now, returned)


def solution(mesh):
    in_specs = (
        P(("atm", "ocn"), None, None),
        P("ocn", None),
        P(("atm", "ocn")),
        P(("atm", "ocn"), None, None),
        P(),
        P(None, "atm", "ocn"),
        P("atm", "ocn"),
    )
    out_specs = (P(None, "atm", "ocn"), P(("atm", "ocn"), None, None))
    return jax.shard_map(body, mesh=mesh, in_specs=in_specs, out_specs=out_specs, check_vma=False)
```

profile of v0, /device:TPU:33, one launch (start us, length us, event | category | flops | bytes accessed | tf_op | source)
XLA Modules:
  0.0 158.0 jit_solution(13683791796724845569)
XLA Ops:
  1.4 4.3 %scatter_custom_fusion = s32[1024]{0:T(1024)S(1)} fusion(s32[1024]{0:T(1024)S(1)} %bitcast.63, s32[1024]{0:T(1024)S(1)} %iota.11, s32[]{:T(128)} %constant.19.clone.1), kind=kCustom, calls=%fused_computation.64 | custom fusion | bytes 4100 | tf_op jit(solution)/shard_map/scatter | solution.py:52
  5.8 1.6 %sort.17 = (s32[32]{0:T(128)}, s32[32]{0:T(128)S(1)}) sort(s32[32]{0:T(128)S(1)} %dynamic_slice.10, s32[32]{0:T(128)S(1)} %iota.12), dimensions={0}, to_apply=%region_1.0 | sort | flops 160 | bytes 512 | tf_op jit(solution)/shard_map/jit(argsort)/sort | solution.py:55
  7.4 1.3 gather_fusion
  8.7 14.9 %all-to-all-start = ((f32[32,16,128]{2,1,0:T(8,128)}), f32[32,16,128]{2,1,0:T(8,128)S(1)}, u32[]{:S(2)}, u32[]{:S(2)}) async-start(f32[32,16,128]{2,1,0:T(8,128)} %gather_fusion), calls=%async_computation | async-start | bytes 524288 | tf_op jit(solution)/shard_map/all_to_all | solution.py:63
  27.2 12.2 %all-to-all-done = f32[32,16,128]{2,1,0:T(8,128)S(1)} async-done(((f32[32,16,128]{2,1,0:T(8,128)}), f32[32,16,128]{2,1,0:T(8,128)S(1)}, u32[]{:S(2)}, u32[]{:S(2)}) %all-to-all-start) | async-done | bytes 262176 | tf_op jit(solution)/shard_map/all_to_all | solution.py:63
  40.6 5.0 %convolution_bitcast_fusion = f32[16,16,256]{2,0,1:T(8,128)} fusion(f32[16,2,16,128]{3,2,1,0:T(8,128)S(1)} %bitcast.59, f32[16,2,128,256]{3,2,1,0:T(8,128)} %bitcast.57), kind=kOutput, calls=%fused_computation.5 | convolution fusion | flops 201326592 | bytes 4718592 | tf_op jit(solution)/shard_map/dkfb,dkbq->fdq/dot_general | solution.py:65
  45.6 13.5 %all-to-all-start.1 = ((f32[16,16,256]{2,0,1:T(8,128)}), f32[16,16,256]{2,0,1:T(8,128)S(1)}, u32[]{:S(2)}, u32[]{:S(2)}) async-start(f32[16,16,256]{2,0,1:T(8,128)} %convolution_bitcast_fusion), calls=%async_computation.1 | async-start | bytes 524288 | tf_op jit(solution)/shard_map/all_to_all | solution.py:66
  59.1 1.9 %collective-permute-start.1 = (f32[4,1,128]{2,0,1:T(4,128)S(1)}, f32[4,1,128]{2,0,1:T(4,128)S(1)}, u32[]{:S(2)}, u32[]{:S(2)}) collective-permute-start(f32[4,1,128]{2,0,1:T(4,128)S(1)} %get-tuple-element.19), channel_id=1, source_target_pairs={{0,16},{16,32},{32,48},{48,64},{64,80},{80,96},{96,112},{112,128},... | collective-permute-start | bytes 6152 | tf_op jit(solution)/shard_map/ppermute | solution.py:18
  61.0 5.5 %collective-permute-start = (f32[4,1,128]{2,0,1:T(4,128)S(1)}, f32[4,1,128]{2,0,1:T(4,128)S(1)}, u32[]{:S(2)}, u32[]{:S(2)}) collective-permute-start(f32[4,1,128]{2,0,1:T(4,128)S(1)} %get-tuple-element.18), channel_id=1, source_target_pairs={{16,0},{32,16},{48,32},{64,48},{80,64},{96,80},{112,96},{128,112},... | collective-permute-start | bytes 6152 | tf_op jit(solution)/shard_map/ppermute | solution.py:19
  66.6 4.3 %collective-permute-done = f32[4,1,128]{2,0,1:T(4,128)S(1)} collective-permute-done((f32[4,1,128]{2,0,1:T(4,128)S(1)}, f32[4,1,128]{2,0,1:T(4,128)S(1)}, u32[]{:S(2)}, u32[]{:S(2)}) %collective-permute-start) | collective-permute-done | bytes 2080 | tf_op jit(solution)/shard_map/ppermute | solution.py:19
  71.0 2.5 %collective-permute-start.2 = (f32[4,34,1]{2,0,1:T(4,128)S(1)}, f32[4,34,1]{2,0,1:T(4,128)S(1)}, u32[]{:S(2)}, u32[]{:S(2)}) collective-permute-start(f32[4,34,1]{2,0,1:T(4,128)S(1)} %get-tuple-element.12), channel_id=1, source_target_pairs={{1,0},{2,1},{3,2},{4,3},{5,4},{6,5},{7,6},{8,7},{9,8},{10,9},{11,1... | collective-permute-start | bytes 1640 | tf_op jit(solution)/shard_map/ppermute | solution.py:19
  73.5 11.9 %collective-permute-start.3 = (f32[4,34,1]{2,0,1:T(4,128)S(1)}, f32[4,34,1]{2,0,1:T(4,128)S(1)}, u32[]{:S(2)}, u32[]{:S(2)}) collective-permute-start(f32[4,34,1]{2,0,1:T(4,128)S(1)} %get-tuple-element.13), channel_id=1, source_target_pairs={{0,1},{1,2},{2,3},{3,4},{4,5},{5,6},{6,7},{7,8},{8,9},{9,10},{10,1... | collective-permute-start | bytes 1640 | tf_op jit(solution)/shard_map/ppermute | solution.py:18
  85.8 1.3 collective-permute-done.3
  87.5 6.0 %collective-permute-start.4 = (f32[4,1,128]{2,0,1:T(4,128)S(1)}, f32[4,1,128]{2,0,1:T(4,128)S(1)}, u32[]{:S(2)}, u32[]{:S(2)}) collective-permute-start(f32[4,1,128]{2,0,1:T(4,128)S(1)} %get-tuple-element.15), channel_id=1, source_target_pairs={{16,0},{32,16},{48,32},{64,48},{80,64},{96,80},{112,96},{128,112},... | collective-permute-start | bytes 6152 | tf_op jit(solution)/shard_map/ppermute | solution.py:19
  93.5 1.9 %collective-permute-start.5 = (f32[4,1,128]{2,0,1:T(4,128)S(1)}, f32[4,1,128]{2,0,1:T(4,128)S(1)}, u32[]{:S(2)}, u32[]{:S(2)}) collective-permute-start(f32[4,1,128]{2,0,1:T(4,128)S(1)} %get-tuple-element.14), channel_id=1, source_target_pairs={{0,16},{16,32},{32,48},{48,64},{64,80},{80,96},{96,112},{112,128},... | collective-permute-start | bytes 6152 | tf_op jit(solution)/shard_map/ppermute | solution.py:18
  95.4 4.5 %collective-permute-done.5 = f32[4,1,128]{2,0,1:T(4,128)S(1)} collective-permute-done((f32[4,1,128]{2,0,1:T(4,128)S(1)}, f32[4,1,128]{2,0,1:T(4,128)S(1)}, u32[]{:S(2)}, u32[]{:S(2)}) %collective-permute-start.5) | collective-permute-done | bytes 2080 | tf_op jit(solution)/shard_map/ppermute | solution.py:18
  100.0 1.9 %collective-permute-start.6 = (f32[4,34,1]{2,0,1:T(4,128)S(1)}, f32[4,34,1]{2,0,1:T(4,128)S(1)}, u32[]{:S(2)}, u32[]{:S(2)}) collective-permute-start(f32[4,34,1]{2,0,1:T(4,128)S(1)} %get-tuple-element.10), channel_id=1, source_target_pairs={{1,0},{2,1},{3,2},{4,3},{5,4},{6,5},{7,6},{8,7},{9,8},{10,9},{11,1... | collective-permute-start | bytes 1640 | tf_op jit(solution)/shard_map/ppermute | solution.py:19
  102.0 14.4 %collective-permute-start.7 = (f32[4,34,1]{2,0,1:T(4,128)S(1)}, f32[4,34,1]{2,0,1:T(4,128)S(1)}, u32[]{:S(2)}, u32[]{:S(2)}) collective-permute-start(f32[4,34,1]{2,0,1:T(4,128)S(1)} %get-tuple-element.11), channel_id=1, source_target_pairs={{0,1},{1,2},{2,3},{3,4},{4,5},{5,6},{6,7},{7,8},{8,9},{9,10},{10,1... | collective-permute-start | bytes 1640 | tf_op jit(solution)/shard_map/ppermute | solution.py:18
  117.2 1.2 collective-permute-done.7
  119.2 16.7 %all-to-all-start.2 = ((f32[4,16,256]{2,0,1:T(4,128)}), f32[4,16,256]{2,0,1:T(4,128)S(1)}, u32[]{:S(2)}, u32[]{:S(2)}) async-start(f32[4,16,256]{2,0,1:T(4,128)} %bitcast.15), calls=%async_computation.2 | async-start | bytes 131072 | tf_op jit(solution)/shard_map/all_to_all | solution.py:75
  135.9 1.5 copy.47
  137.4 13.0 %all-to-all-done.2 = f32[4,16,256]{2,0,1:T(4,128)S(1)} async-done(((f32[4,16,256]{2,0,1:T(4,128)}), f32[4,16,256]{2,0,1:T(4,128)S(1)}, u32[]{:S(2)}, u32[]{:S(2)}) %all-to-all-start.2) | async-done | bytes 65568 | tf_op jit(solution)/shard_map/all_to_all | solution.py:75
  150.4 5.2 %fusion.21 = f32[16,4,2,128]{3,1,2,0:T(4,128)S(1)} fusion(f32[16,2,128,256]{3,2,1,0:T(8,128)} %bitcast.58, f32[4,16,256]{2,0,1:T(4,128)S(1)} %all-to-all-done.2), kind=kOutput, calls=%fused_computation.43 | convolution fusion | flops 50331648 | bytes 4325376 | tf_op jit(solution)/shard_map/cdq,dkbq->dkcb/dot_general | solution.py:76
  155.7 1.6 %scatter_fusion = f32[32,4,128]{2,1,0:T(4,128)S(1)} fusion(f32[32,4,128]{2,1,0:T(4,128)S(1)} %broadcast_in_dim.7, s32[32]{0:T(128)S(1)} %compare_select_fusion.2, f32[32,4,128]{2,1,0:T(4,128)S(1)} %bitcast.60), kind=kCustom, calls=%fused_computation.4 | custom fusion | flops 16384 | bytes 196736 | tf_op jit(solution)/shard_map/scatter-add | solution.py:78
  (56 shorter events, 8.8 us)
Async XLA Ops:
  0.6 6.8 %copy-start = (f32[32,16,128]{2,1,0:T(8,128)S(1)}, f32[32,16,128]{2,1,0:T(8,128)}, u32[]{:S(2)}) copy-start(f32[32,16,128]{2,1,0:T(8,128)} %param.9) | copy-start | bytes 786436
  0.6 65.9 %copy-start.1 = (f32[4,32,128]{2,1,0:T(8,128)S(1)}, f32[4,32,128]{2,1,0:T(8,128)}, u32[]{:S(2)}) copy-start(f32[4,32,128]{2,1,0:T(8,128)} %param.14) | copy-start | bytes 196612
  0.7 84.8 %copy-start.3 = (s32[32,128]{1,0:T(8,128)S(1)}, s32[32,128]{1,0:T(8,128)}, u32[]{:S(2)}) copy-start(s32[32,128]{1,0:T(8,128)} %param.15) | copy-start | bytes 49156
  8.7 30.7 %all-to-all-start = ((f32[32,16,128]{2,1,0:T(8,128)}), f32[32,16,128]{2,1,0:T(8,128)S(1)}, u32[]{:S(2)}, u32[]{:S(2)}) async-start(f32[32,16,128]{2,1,0:T(8,128)} %gather_fusion), calls=%async_computation | async-start | bytes 524288 | tf_op jit(solution)/shard_map/all_to_all | solution.py:63
  23.6 63.4 %copy-start.4 = (f32[4]{0:T(128)S(1)}, f32[4]{0:T(128)}, u32[]{:S(2)}) copy-start(f32[4]{0:T(128)} %constant.50.clone) | copy-start | bytes 52
  23.6 63.4 %copy-start.6 = (f32[4,16]{1,0:T(4,128)S(1)}, f32[4,16]{1,0:T(4,128)}, u32[]{:S(2)}) copy-start(f32[4,16]{1,0:T(4,128)} %param.13) | copy-start | bytes 772
  40.6 95.3 %copy-start.5 = (s32[32]{0:T(128)S(1)}, s32[32]{0:T(128)}, u32[]{:S(2)}) copy-start(s32[32]{0:T(128)} %param.11) | copy-start | bytes 388
  45.6 39.9 %all-to-all-start.1 = ((f32[16,16,256]{2,0,1:T(8,128)}), f32[16,16,256]{2,0,1:T(8,128)S(1)}, u32[]{:S(2)}, u32[]{:S(2)}) async-start(f32[16,16,256]{2,0,1:T(8,128)} %convolution_bitcast_fusion), calls=%async_computation.1 | async-start | bytes 524288 | tf_op jit(solution)/shard_map/all_to_all | solution.py:66
  59.1 7.4 %collective-permute-start.1 = (f32[4,1,128]{2,0,1:T(4,128)S(1)}, f32[4,1,128]{2,0,1:T(4,128)S(1)}, u32[]{:S(2)}, u32[]{:S(2)}) collective-permute-start(f32[4,1,128]{2,0,1:T(4,128)S(1)} %get-tuple-element.19), channel_id=1, source_target_pairs={{0,16},{16,32},{32,48},{48,64},{64,80},{80,96},{96,112},{112,128},... | collective-permute-start | bytes 6152 | tf_op jit(solution)/shard_map/ppermute | solution.py:18
  61.0 9.9 %collective-permute-start = (f32[4,1,128]{2,0,1:T(4,128)S(1)}, f32[4,1,128]{2,0,1:T(4,128)S(1)}, u32[]{:S(2)}, u32[]{:S(2)}) collective-permute-start(f32[4,1,128]{2,0,1:T(4,128)S(1)} %get-tuple-element.18), channel_id=1, source_target_pairs={{16,0},{32,16},{48,32},{64,48},{80,64},{96,80},{112,96},{128,112},... | collective-permute-start | bytes 6152 | tf_op jit(solution)/shard_map/ppermute | solution.py:19
  71.0 14.7 %collective-permute-start.2 = (f32[4,34,1]{2,0,1:T(4,128)S(1)}, f32[4,34,1]{2,0,1:T(4,128)S(1)}, u32[]{:S(2)}, u32[]{:S(2)}) collective-permute-start(f32[4,34,1]{2,0,1:T(4,128)S(1)} %get-tuple-element.12), channel_id=1, source_target_pairs={{1,0},{2,1},{3,2},{4,3},{5,4},{6,5},{7,6},{8,7},{9,8},{10,9},{11,1... | collective-permute-start | bytes 1640 | tf_op jit(solution)/shard_map/ppermute | solution.py:19
  73.5 13.5 %collective-permute-start.3 = (f32[4,34,1]{2,0,1:T(4,128)S(1)}, f32[4,34,1]{2,0,1:T(4,128)S(1)}, u32[]{:S(2)}, u32[]{:S(2)}) collective-permute-start(f32[4,34,1]{2,0,1:T(4,128)S(1)} %get-tuple-element.13), channel_id=1, source_target_pairs={{0,1},{1,2},{2,3},{3,4},{4,5},{5,6},{6,7},{7,8},{8,9},{9,10},{10,1... | collective-permute-start | bytes 1640 | tf_op jit(solution)/shard_map/ppermute | solution.py:18
  87.5 7.9 %collective-permute-start.4 = (f32[4,1,128]{2,0,1:T(4,128)S(1)}, f32[4,1,128]{2,0,1:T(4,128)S(1)}, u32[]{:S(2)}, u32[]{:S(2)}) collective-permute-start(f32[4,1,128]{2,0,1:T(4,128)S(1)} %get-tuple-element.15), channel_id=1, source_target_pairs={{16,0},{32,16},{48,32},{64,48},{80,64},{96,80},{112,96},{128,112},... | collective-permute-start | bytes 6152 | tf_op jit(solution)/shard_map/ppermute | solution.py:19
  93.5 6.4 %collective-permute-start.5 = (f32[4,1,128]{2,0,1:T(4,128)S(1)}, f32[4,1,128]{2,0,1:T(4,128)S(1)}, u32[]{:S(2)}, u32[]{:S(2)}) collective-permute-start(f32[4,1,128]{2,0,1:T(4,128)S(1)} %get-tuple-element.14), channel_id=1, source_target_pairs={{0,16},{16,32},{32,48},{48,64},{64,80},{80,96},{96,112},{112,128},... | collective-permute-start | bytes 6152 | tf_op jit(solution)/shard_map/ppermute | solution.py:18
  100.0 17.1 %collective-permute-start.6 = (f32[4,34,1]{2,0,1:T(4,128)S(1)}, f32[4,34,1]{2,0,1:T(4,128)S(1)}, u32[]{:S(2)}, u32[]{:S(2)}) collective-permute-start(f32[4,34,1]{2,0,1:T(4,128)S(1)} %get-tuple-element.10), channel_id=1, source_target_pairs={{1,0},{2,1},{3,2},{4,3},{5,4},{6,5},{7,6},{8,7},{9,8},{10,9},{11,1... | collective-permute-start | bytes 1640 | tf_op jit(solution)/shard_map/ppermute | solution.py:19
  102.0 16.4 %collective-permute-start.7 = (f32[4,34,1]{2,0,1:T(4,128)S(1)}, f32[4,34,1]{2,0,1:T(4,128)S(1)}, u32[]{:S(2)}, u32[]{:S(2)}) collective-permute-start(f32[4,34,1]{2,0,1:T(4,128)S(1)} %get-tuple-element.11), channel_id=1, source_target_pairs={{0,1},{1,2},{2,3},{3,4},{4,5},{5,6},{6,7},{7,8},{8,9},{9,10},{10,1... | collective-permute-start | bytes 1640 | tf_op jit(solution)/shard_map/ppermute | solution.py:18
  119.2 31.2 %all-to-all-start.2 = ((f32[4,16,256]{2,0,1:T(4,128)}), f32[4,16,256]{2,0,1:T(4,128)S(1)}, u32[]{:S(2)}, u32[]{:S(2)}) async-start(f32[4,16,256]{2,0,1:T(4,128)} %bitcast.15), calls=%async_computation.2 | async-start | bytes 131072 | tf_op jit(solution)/shard_map/all_to_all | solution.py:75
  157.3 0.6 copy-start.2
where the time goes:
time: 159 us; the launch traced here: 158 us
  starting transfers between devices  91.1 us (57%)
  waiting for transfers between devices  37.3 us (23%)
  local copies, waits for them, and re-layouts  11.2 us (7%)
  matrix products  10.7 us (7%)
  other arithmetic  6.68 us (4%)
    ppermute x4, starting transfers between devices, padded_2(): before = lax.ppermute(last, axis, up)  30.2 us
    all_to_all x1, starting transfers between devices, body(): lax.all_to_all(outgoing, 'ocn', split_axis=1, concat_axis=1, tiled=True)  16.7 us
    ppermute x4, starting transfers between devices, padded_2(): after = lax.ppermute(leading, axis, down)  15.9 us
    all_to_all x1, starting transfers between devices, body(): lax.all_to_all(outgoing_blocks, 'atm', split_axis=0, concat_axis=0, tiled...  14.9 us
    all_to_all x1, starting transfers between devices, body(): lax.all_to_all(forcing_rows, 'ocn', split_axis=1, concat_axis=1, tiled=True)  13.5 us
    all_to_all x1, waiting for transfers between devices, body(): lax.all_to_all(outgoing, 'ocn', split_axis=1, concat_axis=1, tiled=True)  13 us
    all_to_all x1, waiting for transfers between devices, body(): lax.all_to_all(outgoing_blocks, 'atm', split_axis=0, concat_axis=0, tiled...  12.2 us
    ppermute x4, waiting for transfers between devices, padded_2(): before = lax.ppermute(last, axis, up)  6.95 us
  transfers between devices with their start and end apart: 11, of which 7 were waited for; matrix products, arithmetic and copies ran while one was open for 3% of the time, Pallas kernels for 0%

commit v1 on v0

v1 whole, which is shorter than its diff:
```python
import functools

import jax
import jax.numpy as jnp
from jax import lax
from jax.experimental import pallas as pl
from jax.experimental.pallas import tpu as pltpu
from jax.sharding import PartitionSpec as P

MESH = pl.DeviceIdType.MESH
F32 = jnp.float32
BF16 = jnp.bfloat16
NSTATE = 4
F = 16
C = 128
HIGHEST = lax.Precision.HIGHEST


def iota(shape, dim):
    return lax.broadcasted_iota(jnp.int32, shape, dim)


def split(x):
    high = x.astype(BF16).astype(F32)
    return jnp.concatenate([high, x - high], axis=0).astype(BF16)


def tend(x, lap, mask, state):
    rows = x.shape[0]
    rot = jnp.where(
        state == 0,
        pltpu.roll(x, rows - 1, 0),
        jnp.where(state == 1, -pltpu.roll(x, 1, 0), 0.0),
    )
    kappa = jnp.where(state < 2, F32(0.8), F32(0.5))
    return mask * (x + 0.25 * (kappa * lap + 0.5 * rot - 0.1 * x))


def kernel(
    na, no,
    atm_h, w_h, st_h, mk_h, cm_v, cm_s, pat_s, c_v,
    on_h, ar_h,
    atm, w32, whi, wlo, st, mk,
    out1, arr1, idx_s,
    row_out, row_in, col_out, col_in,
    mask_out, mask_in, a2_out, a2_in,
    g, g_up, g_dn, on_out, on_in, on_t, back, ar,
    in_sem, w_sem, x_send, x_recv, row_send, row_recv, col_send, col_recv, g_send, g_recv, out_sem,
):
    nb = na
    r4 = NSTATE * nb
    a = lax.axis_index("atm")
    o = lax.axis_index("ocn")
    line = a * no + o

    st_copy = pltpu.make_async_copy(st_h, st, in_sem.at[0])
    mk_copy = pltpu.make_async_copy(mk_h, mk, in_sem.at[1])
    atm_copy = pltpu.make_async_copy(atm_h, atm, in_sem.at[2])
    atm_copy.start()
    st_copy.start()
    mk_copy.start()
    for d in range(no):
        pltpu.make_async_copy(w_h.at[d], w32.at[d], w_sem.at[d]).start()

    barrier = pltpu.get_barrier_semaphore()

    def greet_atm(k, carry):
        pl.semaphore_signal(barrier, inc=1, device_id=(lax.rem(a + k, na), o), device_id_type=MESH)
        return carry

    def greet_ocn(k, carry):
        pl.semaphore_signal(barrier, inc=1, device_id=(a, lax.rem(o + k, no)), device_id_type=MESH)
        return carry

    lax.fori_loop(1, na, greet_atm, 0)
    lax.fori_loop(1, no, greet_ocn, 0)
    cross_up = jnp.logical_and(o == 0, a > 0)
    cross_dn = jnp.logical_and(o == no - 1, a < na - 1)

    @pl.when(cross_up)
    def _():
        pl.semaphore_signal(barrier, inc=1, device_id=(a - 1, no - 1), device_id_type=MESH)

    @pl.when(cross_dn)
    def _():
        pl.semaphore_signal(barrier, inc=1, device_id=(a + 1, 0), device_id_type=MESH)

    slot = iota((r4, na * nb), 1)
    cm = cm_v[...]
    mine = jnp.where(cm // nb == a, (cm % nb).astype(F32), 0.0)
    mine = jnp.where(slot // nb == iota((r4, na * nb), 0) // NSTATE, mine, 0.0)
    order = jnp.sum(mine, axis=1, keepdims=True).astype(jnp.int32)
    coeff = c_v[...]
    coeff = jnp.concatenate([coeff] * 2, axis=0)
    coeff = jnp.concatenate([coeff] * (C // F), axis=1)
    coeff = jnp.concatenate([coeff] * (r4 // 8), axis=0)
    coeff = jnp.concatenate([coeff] * (nb * F // C), axis=1)
    take = jnp.where(order == iota((r4, nb * F), 1) // F, coeff, 0.0)
    atm_copy.wait()
    states = jnp.dot(take, atm[...], precision=HIGHEST, preferred_element_type=F32)
    for b in range(nb):
        out1[b] = states[NSTATE * b : NSTATE * b + NSTATE]
    arr1[a] = out1[a]

    st_copy.wait()
    mk_copy.wait()
    land = mk[...].astype(F32)
    for b in range(no):
        mask_out[b] = land[2 * b : 2 * b + 2]
    mask_in[o] = mask_out[o]
    for s in range(NSTATE):
        a2_out[pl.ds(s, nb, stride=NSTATE), :] = land
    wet = a2_out[...]
    for s in range(NSTATE):
        a2_out[pl.ds(s, nb, stride=NSTATE), :] = st[s]
    tile = a2_out[...]
    state = iota((r4, C), 0) % NSTATE
    lane = iota((r4, C), 1)

    def edges(rnd, x):
        row_out[rnd, 0] = x[:NSTATE]
        row_out[rnd, 1] = x[r4 - NSTATE :]
        turned = x.T
        col_out[rnd, 0] = turned[:1]
        col_out[rnd, 1] = turned[C - 1 :]

    def halo_copies(rnd):
        def row(side, target):
            return pltpu.make_async_remote_copy(
                row_out.at[rnd, side], row_in.at[rnd, 1 - side], row_send.at[rnd, side], row_recv.at[rnd, 1 - side],
                device_id=(target, o), device_id_type=MESH)

        def col(side, target):
            return pltpu.make_async_remote_copy(
                col_out.at[rnd, side], col_in.at[rnd, 1 - side], col_send.at[rnd, side], col_recv.at[rnd, 1 - side],
                device_id=(a, target), device_id_type=MESH)

        return (
            (a > 0, row(0, a - 1)),
            (a < na - 1, row(1, a + 1)),
            (o > 0, col(0, o - 1)),
            (o < no - 1, col(1, o + 1)),
        )

    def start_halo(rnd):
        for there, copy in halo_copies(rnd):
            @pl.when(there)
            def _():
                copy.start()

    def wait_halo_send(rnd):
        for there, copy in halo_copies(rnd):
            @pl.when(there)
            def _():
                copy.wait_send()

    def wait_halo_recv(rnd):
        for side, there, neighbour in ((0, a > 0, a - 1), (1, a < na - 1, a + 1)):
            @pl.when(there)
            def _():
                pltpu.make_async_remote_copy(
                    row_out.at[rnd, side], row_in.at[rnd, side], row_send.at[rnd, side], row_recv.at[rnd, side],
                    device_id=(neighbour, o), device_id_type=MESH).wait_recv()
        for side, there, neighbour in ((0, o > 0, o - 1), (1, o < no - 1, o + 1)):
            @pl.when(there)
            def _():
                pltpu.make_async_remote_copy(
                    col_out.at[rnd, side], col_in.at[rnd, side], col_send.at[rnd, side], col_recv.at[rnd, side],
                    device_id=(a, neighbour), device_id_type=MESH).wait_recv()

    for side, outside in ((0, a == 0), (1, a == na - 1)):
        @pl.when(outside)
        def _():
            row_in[0, side] = jnp.zeros((NSTATE, C), F32)
            row_in[1, side] = jnp.zeros((NSTATE, C), F32)

    for side, outside in ((0, o == 0), (1, o == no - 1)):
        @pl.when(outside)
        def _():
            col_in[0, side] = jnp.zeros((1, r4), F32)
            col_in[1, side] = jnp.zeros((1, r4), F32)

    @pl.when(line == 0)
    def _():
        g_up[...] = jnp.zeros_like(g_up)

    @pl.when(line == na * no - 1)
    def _():
        g_dn[...] = jnp.zeros_like(g_dn)

    def substep(rnd, x):
        up = jnp.concatenate([row_in[rnd, 0], x[: r4 - NSTATE]], axis=0)
        down = jnp.concatenate([x[NSTATE:], row_in[rnd, 1]], axis=0)
        at = iota((C, r4), 0)
        beside = jnp.where(at == 0, col_in[rnd, 0], jnp.where(at == C - 1, col_in[rnd, 1], 0.0)).T
        left = jnp.where(lane == 0, beside, pltpu.roll(x, 1, 1))
        right = jnp.where(lane == C - 1, beside, pltpu.roll(x, C - 1, 1))
        return tend(x, up + down + left + right - 4.0 * x, wet, state)

    edges(0, tile)
    pl.semaphore_wait(barrier, na + no - 2 + cross_up.astype(jnp.int32) + cross_dn.astype(jnp.int32))

    def send_block(k, carry):
        to = lax.rem(a + k, na)
        pltpu.make_async_remote_copy(
            out1.at[to], arr1.at[a], x_send.at[0], x_recv.at[0], device_id=(to, o), device_id_type=MESH).start()
        return carry

    lax.fori_loop(1, na, send_block, 0)
    start_halo(0)

    def send_mask(k, carry):
        to = lax.rem(o + k, no)
        pltpu.make_async_remote_copy(
            mask_out.at[to], mask_in.at[o], x_send.at[1], x_recv.at[1], device_id=(a, to), device_id_type=MESH).start()
        return carry

    lax.fori_loop(1, no, send_mask, 0)

    for r in range(nb):
        idx_s[r] = cm_s[0, a * nb + pat_s[r]] // nb

    def split_weights(d, carry):
        pltpu.make_async_copy(w_h.at[d], w32.at[d], w_sem.at[d]).wait()
        w = w32[d]
        high = w.astype(BF16)
        whi[d] = high
        wlo[d] = (w - high.astype(F32)).astype(BF16)
        return carry

    lax.fori_loop(0, no, split_weights, 0)

    wait_halo_recv(0)
    tile = substep(0, tile)
    edges(1, tile)
    start_halo(1)
    wait_halo_recv(1)
    a2_out[...] = substep(1, tile)

    def rows_of(d):
        return pl.ds(pl.multiple_of(8 * d, 8), 8)

    a2_in[rows_of(o)] = a2_out[rows_of(o)]

    def send_a2(k, carry):
        to = lax.rem(o + k, no)
        pltpu.make_async_remote_copy(
            a2_out.at[rows_of(to)], a2_in.at[rows_of(o)], x_send.at[2], x_recv.at[2],
            device_id=(a, to), device_id_type=MESH).start()
        return carry

    lax.fori_loop(1, no, send_a2, 0)

    def wait_all(i, ref, count, send):
        part = ref.at[pl.ds(0, count)]
        copy = pltpu.make_async_remote_copy(
            part, part, x_send.at[i], x_recv.at[i], device_id=(a, o), device_id_type=MESH)
        if send:
            copy.wait_send()
        else:
            copy.wait_recv()

    wait_all(1, mask_in, no - 1, False)
    wait_all(0, arr1, nb - 1, False)
    for d in range(no):
        x = jnp.concatenate([arr1[idx_s[2 * d]], arr1[idx_s[2 * d + 1]]], axis=1)
        x = split(x)
        f = jnp.dot(x, whi[d], preferred_element_type=F32) + jnp.dot(x, wlo[d], preferred_element_type=F32)
        f = 0.25 * (f[:NSTATE] + f[NSTATE:])
        g[0, d] = f[:, :C] * mask_in[d, 0:1]
        g[1, d] = f[:, C:] * mask_in[d, 1:2]

    above = ((line - 1) // no, (line - 1) % no)
    below = ((line + 1) // no, (line + 1) % no)

    @pl.when(line > 0)
    def _():
        pltpu.make_async_remote_copy(
            g.at[0], g_dn, g_send.at[0], g_recv.at[1], device_id=above, device_id_type=MESH).start()

    @pl.when(line < na * no - 1)
    def _():
        pltpu.make_async_remote_copy(
            g.at[1], g_up, g_send.at[1], g_recv.at[0], device_id=below, device_id_type=MESH).start()

    wait_all(2, a2_in, 8 * (no - 1), False)

    @pl.when(line > 0)
    def _():
        pltpu.make_async_remote_copy(
            g.at[0], g_up, g_send.at[0], g_recv.at[0], device_id=above, device_id_type=MESH).wait_recv()

    @pl.when(line < na * no - 1)
    def _():
        pltpu.make_async_remote_copy(
            g.at[1], g_dn, g_send.at[1], g_recv.at[1], device_id=below, device_id_type=MESH).wait_recv()

    state8 = iota((8, C), 0) % NSTATE
    lane8 = iota((8, C), 1)
    rows = [jnp.concatenate([g[0, d], g[1, d]], axis=0) for d in range(no)]
    lefts = [pltpu.roll(x, 1, 1) for x in rows]
    rights = [pltpu.roll(x, C - 1, 1) for x in rows]
    nothing = jnp.zeros((8, C), F32)
    for d in range(no):
        x = rows[d]
        up = jnp.concatenate([g_up[d], x[:NSTATE]], axis=0)
        down = jnp.concatenate([x[NSTATE:], g_dn[d]], axis=0)
        left = jnp.where(lane8 == 0, lefts[d - 1] if d > 0 else nothing, lefts[d])
        right = jnp.where(lane8 == C - 1, rights[d + 1] if d < no - 1 else nothing, rights[d])
        wet8 = jnp.where(iota((8, C), 0) < NSTATE, mask_in[d, 0:1], mask_in[d, 1:2])
        on_out[8 * d : 8 * d + 8] = a2_in[8 * d : 8 * d + 8] + (x + tend(x, up + down + left + right - 4.0 * x, wet8, state8))

    on_in[rows_of(o)] = on_out[rows_of(o)]

    def send_on(k, carry):
        to = lax.rem(o + k, no)
        pltpu.make_async_remote_copy(
            on_out.at[rows_of(to)], on_in.at[rows_of(o)], x_send.at[3], x_recv.at[3],
            device_id=(a, to), device_id_type=MESH).start()
        return carry

    lax.fori_loop(1, no, send_on, 0)

    nt = (((1,), (1,)), ((), ()))
    for d in range(no):
        x = on_out[8 * d : 8 * d + 8]
        x = split(jnp.concatenate([x[:NSTATE], x[NSTATE:]], axis=1))
        f = lax.dot_general(x, whi[d], nt, preferred_element_type=F32) + lax.dot_general(
            x, wlo[d], nt, preferred_element_type=F32)
        f = f[:NSTATE] + f[NSTATE:]
        back[8 * d : 8 * d + 8] = jnp.concatenate([f[:, :C], f[:, C:]], axis=0)

    across = iota((r4, r4), 1)
    along = iota((r4, r4), 0)
    pattern = jnp.zeros((1, r4), jnp.int32)
    for r in range(nb):
        pattern = jnp.where(iota((1, r4), 1) // NSTATE == r, pat_s[r], pattern)
    place = jnp.logical_and(pattern == along // NSTATE, across % NSTATE == along % NSTATE)
    placed = jnp.dot(jnp.where(place, 1.0, 0.0).astype(F32), back[...], precision=HIGHEST, preferred_element_type=F32)
    for b in range(nb):
        ar[b] = placed[NSTATE * b : NSTATE * b + NSTATE]
    ar_copy = pltpu.make_async_copy(ar, ar_h, out_sem.at[0])
    ar_copy.start()

    wait_all(3, on_in, 8 * (no - 1), False)
    for s in range(NSTATE):
        on_t[s] = on_in[pl.ds(s, nb, stride=NSTATE), :]
    on_copy = pltpu.make_async_copy(on_t, on_h, out_sem.at[1])
    on_copy.start()

    wait_all(0, out1, nb - 1, True)
    wait_all(1, mask_out, no - 1, True)
    wait_all(2, a2_out, 8 * (no - 1), True)
    wait_all(3, on_out, 8 * (no - 1), True)
    wait_halo_send(0)
    wait_halo_send(1)

    @pl.when(line > 0)
    def _():
        pltpu.make_async_remote_copy(
            g.at[0], g_dn, g_send.at[0], g_recv.at[1], device_id=above, device_id_type=MESH).wait_send()

    @pl.when(line < na * no - 1)
    def _():
        pltpu.make_async_remote_copy(
            g.at[1], g_up, g_send.at[1], g_recv.at[0], device_id=below, device_id_type=MESH).wait_send()

    ar_copy.wait()
    on_copy.wait()


def body(na, no, atm_fields, coupler_map, remap_pattern, remap_weights, bulk_coeffs, ocean_state, land_mask):
    nb = atm_fields.shape[0]
    r4 = NSTATE * nb
    any_space = pl.BlockSpec(memory_space=pl.ANY)
    vmem = pl.BlockSpec(memory_space=pltpu.VMEM)
    smem = pl.BlockSpec(memory_space=pltpu.SMEM)
    dma = pltpu.SemaphoreType.DMA
    return pl.pallas_call(
        functools.partial(kernel, na, no),
        out_shape=(
            jax.ShapeDtypeStruct(ocean_state.shape, F32),
            jax.ShapeDtypeStruct((nb, NSTATE, C), F32),
        ),
        in_specs=[any_space, any_space, any_space, any_space, vmem, smem, smem, vmem],
        out_specs=(any_space, any_space),
        scratch_shapes=[
            pltpu.VMEM((nb * F, C), F32),
            pltpu.VMEM((no, 2 * C, 2 * C), F32),
            pltpu.VMEM((no, 2 * C, 2 * C), BF16),
            pltpu.VMEM((no, 2 * C, 2 * C), BF16),
            pltpu.VMEM((NSTATE, nb, C), F32),
            pltpu.VMEM((nb, C), jnp.int32),
            pltpu.VMEM((nb, NSTATE, C), F32),
            pltpu.VMEM((nb, NSTATE, C), F32),
            pltpu.SMEM((nb,), jnp.int32),
            pltpu.VMEM((2, 2, NSTATE, C), F32),
            pltpu.VMEM((2, 2, NSTATE, C), F32),
            pltpu.VMEM((2, 2, 1, r4), F32),
            pltpu.VMEM((2, 2, 1, r4), F32),
            pltpu.VMEM((no, 2, C), F32),
            pltpu.VMEM((no, 2, C), F32),
            pltpu.VMEM((r4, C), F32),
            pltpu.VMEM((r4, C), F32),
            pltpu.VMEM((2, no, NSTATE, C), F32),
            pltpu.VMEM((no, NSTATE, C), F32),
            pltpu.VMEM((no, NSTATE, C), F32),
            pltpu.VMEM((r4, C), F32),
            pltpu.VMEM((r4, C), F32),
            pltpu.VMEM((NSTATE, nb, C), F32),
            pltpu.VMEM((r4, C), F32),
            pltpu.VMEM((nb, NSTATE, C), F32),
            dma((3,)),
            dma((no,)),
            dma((4,)),
            dma((4,)),
            dma((2, 2)),
            dma((2, 2)),
            dma((2, 2)),
            dma((2, 2)),
            dma((2,)),
            dma((2,)),
            dma((2,)),
        ],
        compiler_params=pltpu.CompilerParams(
            collective_id=0, has_side_effects=True, vmem_limit_bytes=32 * 1024 * 1024
        ),
    )(
        atm_fields.reshape(nb * F, C),
        remap_weights.reshape(no, 2 * C, 2 * C),
        ocean_state,
        land_mask,
        coupler_map,
        coupler_map,
        remap_pattern,
        bulk_coeffs,
    )


def solution(mesh):
    in_specs = (
        P(("atm", "ocn"), None, None),
        P("ocn", None),
        P(("atm", "ocn")),
        P(("atm", "ocn"), None, None),
        P(),
        P(None, "atm", "ocn"),
        P("atm", "ocn"),
    )
    out_specs = (P(None, "atm", "ocn"), P(("atm", "ocn"), None, None))
    step = functools.partial(body, mesh.shape["atm"], mesh.shape["ocn"])
    return jax.shard_map(step, mesh=mesh, in_specs=in_specs, out_specs=out_specs, check_vma=False)
```

time: 159 us -> 62.8 us (0.39)
  the two profiles are of different devices: /device:TPU:33 before, /device:TPU:1 now
where the time goes in v1:
time: 62.8 us; the launch traced here: 62.5 us
  Pallas kernels  53.8 us (86%)
  local copies, waits for them, and re-layouts  7.97 us (13%)
  between operations  0.66 us (1%)
    pallas_call x1, Pallas kernels, body(): pl.pallas_call(functools.partial(kernel, na, no), out_shape=(jax.ShapeDty...  53.8 us
    unnamed x16, local copies, waits for them, and re-layouts  7.97 us

profile of v1, /device:TPU:1, one launch (start us, length us, event | category | flops | bytes accessed | tf_op | source)
XLA Modules:
  0.0 62.5 jit_solution(3211733984150433154)
XLA Ops:
  0.6 0.0 copy-start
  0.6 2.2 %copy-done = f32[32,128,256]{2,1,0:T(8,128)S(1)} copy-done((f32[32,128,256]{2,1,0:T(8,128)S(1)}, f32[32,128,256]{2,1,0:T(8,128)}, u32[]{:S(2)}) %copy-start) | copy-done | bytes 4194328
  2.8 0.0 copy-start.1
  2.8 0.9 %copy-done.1 = f32[32,16,128]{2,1,0:T(8,128)S(1)} copy-done((f32[32,16,128]{2,1,0:T(8,128)S(1)}, f32[32,16,128]{2,1,0:T(8,128)}, u32[]{:S(2)}) %copy-start.1) | copy-done | bytes 262168
  3.8 0.0 copy-start.2
  3.8 0.8 %copy-done.2 = f32[4,32,128]{2,1,0:T(8,128)S(1)} copy-done((f32[4,32,128]{2,1,0:T(8,128)S(1)}, f32[4,32,128]{2,1,0:T(8,128)}, u32[]{:S(2)}) %copy-start.2) | copy-done | bytes 65560
  4.6 0.0 copy-start.3
  4.6 0.7 %copy-done.3 = s32[32,128]{1,0:T(8,128)S(1)} copy-done((s32[32,128]{1,0:T(8,128)S(1)}, s32[32,128]{1,0:T(8,128)}, u32[]{:S(2)}) %copy-start.3) | copy-done | bytes 16408
  5.3 0.0 copy-start.4
  5.3 0.7 %copy-done.4 = s32[1,1024]{1,0:T(1,128)S(1)} copy-done((s32[1,1024]{1,0:T(1,128)S(1)}, s32[1,1024]{1,0:T(1,128)}, u32[]{:S(2)}) %copy-start.4) | copy-done | bytes 4120
  6.0 0.0 copy-start.5
  6.0 0.7 %copy-done.5 = f32[4,16]{1,0:T(4,128)S(1)} copy-done((f32[4,16]{1,0:T(4,128)S(1)}, f32[4,16]{1,0:T(4,128)}, u32[]{:S(2)}) %copy-start.5) | copy-done | bytes 280
  6.7 0.0 copy-start.6
  6.7 0.7 %copy-done.6 = s32[32]{0:T(128)S(1)} copy-done((s32[32]{0:T(128)S(1)}, s32[32]{0:T(128)}, u32[]{:S(2)}) %copy-start.6) | copy-done | bytes 152
  7.4 53.8 %shard_map.86 = (f32[4,32,128]{2,1,0:T(8,128)S(1)}, f32[32,4,128]{2,1,0:T(4,128)S(1)}) custom-call(f32[512,128]{1,0:T(8,128)S(1)} %bitcast.3, f32[16,256,256]{2,1,0:T(8,128)S(1)} %bitcast.2, f32[4,32,128]{2,1,0:T(8,128)S(1)} %copy-done.2, s32[32,128]{1,0:T(8,128)S(1)} %copy-done.3, s32[1,1024]{1,0:T(1,128)S(1)} %copy-done.4, s32[1,1024]{1,0:T(1,128)S(1)} %copy-done.4, ...), custom_call_target="tpu_custom_call" | custom-call | tf_op jit(solution)/shard_map/pallas_call | solution.py:379
  61.2 0.6 %copy.11 = f32[4,32,128]{2,1,0:T(8,128)} copy(f32[4,32,128]{2,1,0:T(8,128)S(1)} %get-tuple-element.4) | data formatting | bytes 131072
  61.8 0.6 %copy.12 = f32[32,4,128]{2,1,0:T(4,128)} copy(f32[32,4,128]{2,1,0:T(4,128)S(1)} %get-tuple-element.5) | data formatting | bytes 131072
Async XLA Ops:
  0.6 2.2 %copy-start = (f32[32,128,256]{2,1,0:T(8,128)S(1)}, f32[32,128,256]{2,1,0:T(8,128)}, u32[]{:S(2)}) copy-start(f32[32,128,256]{2,1,0:T(8,128)} %param.10) | copy-start | bytes 12582916
  2.8 0.9 %copy-start.1 = (f32[32,16,128]{2,1,0:T(8,128)S(1)}, f32[32,16,128]{2,1,0:T(8,128)}, u32[]{:S(2)}) copy-start(f32[32,16,128]{2,1,0:T(8,128)} %param.7) | copy-start | bytes 786436
  3.8 0.8 %copy-start.2 = (f32[4,32,128]{2,1,0:T(8,128)S(1)}, f32[4,32,128]{2,1,0:T(8,128)}, u32[]{:S(2)}) copy-start(f32[4,32,128]{2,1,0:T(8,128)} %st_h.1) | copy-start | bytes 196612
  4.6 0.7 %copy-start.3 = (s32[32,128]{1,0:T(8,128)S(1)}, s32[32,128]{1,0:T(8,128)}, u32[]{:S(2)}) copy-start(s32[32,128]{1,0:T(8,128)} %mk_h.1) | copy-start | bytes 49156
  5.3 0.7 %copy-start.4 = (s32[1,1024]{1,0:T(1,128)S(1)}, s32[1,1024]{1,0:T(1,128)}, u32[]{:S(2)}) copy-start(s32[1,1024]{1,0:T(1,128)} %cm_s.1) | copy-start | bytes 12292
  6.0 0.7 %copy-start.5 = (f32[4,16]{1,0:T(4,128)S(1)}, f32[4,16]{1,0:T(4,128)}, u32[]{:S(2)}) copy-start(f32[4,16]{1,0:T(4,128)} %c_v.1) | copy-start | bytes 772
  6.7 0.7 %copy-start.6 = (s32[32]{0:T(128)S(1)}, s32[32]{0:T(128)}, u32[]{:S(2)}) copy-start(s32[32]{0:T(128)} %pat_s.1) | copy-start | bytes 388

commit v2 on v1

v2 whole, which is shorter than its diff:
```python
import functools

import jax
import jax.numpy as jnp
from jax import lax
from jax.experimental import pallas as pl
from jax.experimental.pallas import tpu as pltpu
from jax.sharding import PartitionSpec as P

MESH = pl.DeviceIdType.MESH
F32 = jnp.float32
BF16 = jnp.bfloat16
NSTATE = 4
F = 16
C = 128
HIGHEST = lax.Precision.HIGHEST


def iota(shape, dim):
    return lax.broadcasted_iota(jnp.int32, shape, dim)


def split(x):
    high = x.astype(BF16).astype(F32)
    return jnp.concatenate([high, x - high], axis=0).astype(BF16)


def tend(x, lap, mask, state):
    rows = x.shape[0]
    rot = jnp.where(
        state == 0,
        pltpu.roll(x, rows - 1, 0),
        jnp.where(state == 1, -pltpu.roll(x, 1, 0), 0.0),
    )
    kappa = jnp.where(state < 2, F32(0.8), F32(0.5))
    return mask * (x + 0.25 * (kappa * lap + 0.5 * rot - 0.1 * x))


def kernel(
    na, no,
    atm_h, w_h, st_h, mk_h, cm_h, pat_h, c_h,
    on_h, ar_h,
    cm_v, cm_s, pat_s, c_v,
    atm, w32, whi, wlo, st, mk,
    out1, arr1, idx_s,
    row_out, row_in, col_out, col_in,
    mask_out, mask_in, a2_out, a2_in,
    g, g_up, g_dn, gx, g_in, edge_out, edge_in, g_halo, on_t, back, ar,
    in_sem, w_sem, x_send, x_recv, row_send, row_recv, col_send, col_recv, g_send, g_recv, h_send, h_recv, out_sem,
):
    nb = na
    r4 = NSTATE * nb
    a = lax.axis_index("atm")
    o = lax.axis_index("ocn")
    line = a * no + o

    nz = na // 4
    half = (a // 4) // (nz // 2)
    nx = no // 4

    def atm_peer(k):
        i = k // 4
        return (i * half + (nz - 1 - i) * (1 - half)) * 4 + k % 4

    def ocn_peer(k):
        rest = k % (no // 2)
        x = (o // 4 + rest // 2 + nx // 2) % nx
        z = (o // 2 + 1 + k // (no // 2)) % 2
        return x * 4 + z * 2 + (o + rest) % 2

    def each(count, peer, me, act):
        def step(k, carry):
            to = peer(k)

            @pl.when(to != me)
            def _():
                act(to)

            return carry

        lax.fori_loop(0, count, step, 0)

    barrier = pltpu.get_barrier_semaphore()

    def greet(device):
        pl.semaphore_signal(barrier, inc=1, device_id=device, device_id_type=MESH)

    each(no, ocn_peer, o, lambda to: greet((a, to)))
    each(na, atm_peer, a, lambda to: greet((to, o)))
    has_up, has_dn, has_left, has_right = a > 0, a < na - 1, o > 0, o < no - 1
    corners = []
    for dv, vert in ((-1, has_up), (1, has_dn)):
        @pl.when(vert)
        def _():
            greet((a + dv, no - 1 if dv < 0 else 0))

        for dh, hori in ((-1, has_left), (1, has_right)):
            corners.append((dv, dh, jnp.logical_and(vert, hori)))

            @pl.when(corners[-1][2])
            def _():
                greet((a + dv, o + dh))

    first = jnp.logical_and(o == 0, has_up)
    last = jnp.logical_and(o == no - 1, has_dn)
    greetings = na + no - 2 + no * (first.astype(jnp.int32) + last.astype(jnp.int32))
    for _, _, there in corners:
        greetings += there.astype(jnp.int32)

    copies = [
        pltpu.make_async_copy(src, dst, in_sem.at[i])
        for i, (src, dst) in enumerate((
            (cm_h, cm_v), (c_h, c_v), (atm_h, atm), (st_h, st), (mk_h, mk), (cm_h, cm_s), (pat_h, pat_s)))
    ]
    for copy in copies:
        copy.start()
    for d in range(no):
        pltpu.make_async_copy(w_h.at[d], w32.at[d], w_sem.at[d]).start()

    copies[0].wait()
    copies[1].wait()
    slot = iota((r4, na * nb), 1)
    cm = cm_v[...]
    mine = jnp.where(cm // nb == a, (cm % nb).astype(F32), 0.0)
    mine = jnp.where(slot // nb == iota((r4, na * nb), 0) // NSTATE, mine, 0.0)
    order = jnp.sum(mine, axis=1, keepdims=True).astype(jnp.int32)
    coeff = c_v[...]
    coeff = jnp.concatenate([coeff] * 2, axis=0)
    coeff = jnp.concatenate([coeff] * (C // F), axis=1)
    coeff = jnp.concatenate([coeff] * (r4 // 8), axis=0)
    coeff = jnp.concatenate([coeff] * (nb * F // C), axis=1)
    take = jnp.where(order == iota((r4, nb * F), 1) // F, coeff, 0.0)
    copies[2].wait()
    states = jnp.dot(take, atm[...], precision=HIGHEST, preferred_element_type=F32)
    for b in range(nb):
        out1[b] = states[NSTATE * b : NSTATE * b + NSTATE]
    arr1[a] = out1[a]

    copies[3].wait()
    copies[4].wait()
    land = mk[...].astype(F32)
    for b in range(no):
        mask_out[b] = land[2 * b : 2 * b + 2]
    mask_in[o] = mask_out[o]
    for s in range(NSTATE):
        a2_out[pl.ds(s, nb, stride=NSTATE), :] = land
    wet = a2_out[...]
    for s in range(NSTATE):
        a2_out[pl.ds(s, nb, stride=NSTATE), :] = st[s]
    tile = a2_out[...]
    turned, wet_turned = tile.T, wet.T
    for i in range(2):
        row_out[0, i] = tile[NSTATE * i : NSTATE * i + NSTATE]
        row_out[1, i] = tile[r4 - NSTATE * i - NSTATE : r4 - NSTATE * i]
        col_out[0, i : i + 1] = turned[i : i + 1]
        col_out[1, i : i + 1] = turned[C - 1 - i : C - i]
    row_out[0, 2] = wet[:NSTATE]
    row_out[1, 2] = wet[r4 - NSTATE :]
    col_out[0, 2:3] = wet_turned[:1]
    col_out[1, 2:3] = wet_turned[C - 1 :]
    for side in range(2):
        col_out[side, 3:4] = jnp.zeros((1, r4), F32)

    def row_copy(side, up_or_down, target):
        return pltpu.make_async_remote_copy(
            row_out.at[side], row_in.at[up_or_down], row_send.at[side], row_recv.at[up_or_down],
            device_id=(target, o), device_id_type=MESH)

    def col_copy(side, place, flight, target):
        return pltpu.make_async_remote_copy(
            col_out.at[side], col_in.at[place], col_send.at[flight], col_recv.at[place],
            device_id=target, device_id_type=MESH)

    halos = [
        (has_left, col_copy(0, 3, 2, (a, o - 1)), col_copy(0, 2, 2, (a, o - 1))),
        (has_right, col_copy(1, 2, 3, (a, o + 1)), col_copy(1, 3, 3, (a, o + 1))),
    ]
    for dv, dh, there in corners:
        side = 0 if dh < 0 else 1
        here = (0 if dv < 0 else 4) + side
        halos.append((there, col_copy(side, 5 - here, here, (a + dv, o + dh)), col_copy(side, here, here, (a + dv, o + dh))))
    halos.append((has_up, row_copy(0, 1, a - 1), row_copy(0, 0, a - 1)))
    halos.append((has_dn, row_copy(1, 0, a + 1), row_copy(1, 1, a + 1)))

    for side, inside in ((0, has_up), (1, has_dn)):
        @pl.when(jnp.logical_not(inside))
        def _():
            row_in[side] = jnp.zeros((3, NSTATE, C), F32)
            g_halo[side] = jnp.zeros((NSTATE, C), F32)

    places = [(2, has_left), (3, has_right)]
    places += [((0 if dv < 0 else 4) + (0 if dh < 0 else 1), there) for dv, dh, there in corners]
    for place, inside in places:
        @pl.when(jnp.logical_not(inside))
        def _():
            col_in[place] = jnp.zeros((4, r4), F32)

    has_above, has_below = line > 0, line < na * no - 1

    @pl.when(jnp.logical_not(has_above))
    def _():
        g_up[...] = jnp.zeros_like(g_up)

    @pl.when(jnp.logical_not(has_below))
    def _():
        g_dn[...] = jnp.zeros_like(g_dn)

    def block_copy(to):
        return pltpu.make_async_remote_copy(
            out1.at[to], arr1.at[a], x_send.at[0], x_recv.at[0], device_id=(to, o), device_id_type=MESH)

    def ocn_copy(i, src, dst, to):
        return pltpu.make_async_remote_copy(
            src, dst, x_send.at[i], x_recv.at[i], device_id=(a, to), device_id_type=MESH)

    def rows_of(d):
        return pl.ds(pl.multiple_of(8 * d, 8), 8)

    pl.semaphore_wait(barrier, greetings)
    each(na, atm_peer, a, lambda to: block_copy(to).start())
    for there, copy, _ in halos:
        @pl.when(there)
        def _():
            copy.start()

    each(no, ocn_peer, o, lambda to: ocn_copy(1, mask_out.at[to], mask_in.at[o], to).start())

    copies[5].wait()
    copies[6].wait()
    for r in range(nb):
        idx_s[r] = cm_s[0, a * nb + pat_s[r]] // nb

    def split_weights(d, carry):
        pltpu.make_async_copy(w_h.at[d], w32.at[d], w_sem.at[d]).wait()
        w = w32[d]
        high = w.astype(BF16)
        whi[d] = high
        wlo[d] = (w - high.astype(F32)).astype(BF16)
        return carry

    lax.fori_loop(0, no, split_weights, 0)
    across = iota((r4, r4), 1)
    along = iota((r4, r4), 0)
    pattern = jnp.zeros((1, r4), jnp.int32)
    for r in range(nb):
        pattern = jnp.where(iota((1, r4), 1) // NSTATE == r, pat_s[r], pattern)
    place = jnp.logical_and(pattern == along // NSTATE, across % NSTATE == along % NSTATE)
    place = jnp.where(place, 1.0, 0.0).astype(F32)

    for there, _, copy in halos:
        @pl.when(there)
        def _():
            copy.wait_recv()

    at, along_lane = iota((C, r4), 0), iota((C, r4), 1)
    beside = jnp.zeros((C, r4), F32)
    for i in range(3):
        beside = jnp.where(at == i, col_in[3, i : i + 1], beside)
        beside = jnp.where(at == C - 1 - i, col_in[2, i : i + 1], beside)
    diagonal = jnp.where(
        at == 0,
        jnp.where(along_lane < r4 // 2, col_in[5, :1], col_in[1, :1]),
        jnp.where(at == C - 1, jnp.where(along_lane < r4 // 2, col_in[4, :1], col_in[0, :1]), 0.0))
    beside, diagonal = beside.T, diagonal.T
    rows = r4 + 4 * NSTATE
    lane = iota((rows, C), 1)
    state = iota((rows, C), 0) % NSTATE
    none = jnp.zeros((NSTATE, C), F32)
    x = jnp.concatenate([row_in[0, 1], row_in[0, 0], tile, row_in[1, 0], row_in[1, 1]], axis=0)
    e = jnp.concatenate([none, diagonal[r4 - NSTATE :], beside, diagonal[:NSTATE], none], axis=0)
    wet_x = jnp.concatenate([none, row_in[0, 2], wet, row_in[1, 2], none], axis=0)
    wet_e = jnp.concatenate([none, none, beside, none, none], axis=0)
    wet_e = jnp.where(lane == 0, pltpu.roll(wet_e, C - 2, 1), jnp.where(lane == C - 1, pltpu.roll(wet_e, 2, 1), 0.0))

    def sides(x, e):
        x_right, e_right = pltpu.roll(x, 1, 1), pltpu.roll(e, 1, 1)
        x_left, e_left = pltpu.roll(x, C - 1, 1), pltpu.roll(e, C - 1, 1)
        low, high = iota(x.shape, 1) == 0, iota(x.shape, 1) == C - 1
        of_x = jnp.where(low, e_right, x_right) + jnp.where(high, e_left, x_left)
        of_e = jnp.where(low, x_right, e_right) + jnp.where(high, x_left, e_left)
        return of_x, of_e

    def rises(x):
        return pltpu.roll(x, NSTATE, 0) + pltpu.roll(x, rows - NSTATE, 0)

    of_x, of_e = sides(x, e)
    x, e = tend(x, rises(x) + of_x - 4.0 * x, wet_x, state), tend(e, rises(e) + of_e - 4.0 * e, wet_e, state)
    of_x, _ = sides(x, e)
    x = tend(x, rises(x) + of_x - 4.0 * x, wet_x, state)
    a2_out[...] = x[2 * NSTATE : 2 * NSTATE + r4]
    a2_in[rows_of(o)] = a2_out[rows_of(o)]
    each(no, ocn_peer, o, lambda to: ocn_copy(2, a2_out.at[rows_of(to)], a2_in.at[rows_of(o)], to).start())

    def wait_all(i, ref, count, send):
        part = ref.at[pl.ds(0, count)]
        copy = ocn_copy(i, part, part, o)
        if send:
            copy.wait_send()
        else:
            copy.wait_recv()

    wait_all(1, mask_in, no - 1, False)
    wait_all(0, arr1, nb - 1, False)
    pairs = []
    for d in range(no):
        x = jnp.concatenate([arr1[idx_s[2 * d]], arr1[idx_s[2 * d + 1]]], axis=1)
        x = split(x)
        f = jnp.dot(x, whi[d], preferred_element_type=F32) + jnp.dot(x, wlo[d], preferred_element_type=F32)
        f = 0.25 * (f[:NSTATE] + f[NSTATE:])
        upper, lower = f[:, :C] * mask_in[d, 0:1], f[:, C:] * mask_in[d, 1:2]
        g[0, d] = upper
        g[1, d] = lower
        pairs.append(jnp.concatenate([upper, lower], axis=0))
        gx[8 * d : 8 * d + 8] = pairs[d]

        @pl.when(o != d)
        def _():
            ocn_copy(3, gx.at[pl.ds(8 * d, 8)], g_in.at[rows_of(o)], d).start()

    g_in[rows_of(o)] = gx[rows_of(o)]
    above = ((line - 1) // no, (line - 1) % no)
    below = ((line + 1) // no, (line + 1) % no)

    def g_copy(row, dst, place, target):
        return pltpu.make_async_remote_copy(
            g.at[row], dst, g_send.at[row], g_recv.at[place], device_id=target, device_id_type=MESH)

    @pl.when(has_above)
    def _():
        g_copy(0, g_dn, 1, above).start()

    @pl.when(has_below)
    def _():
        g_copy(1, g_up, 0, below).start()

    lane8, row8 = iota((8, C), 1), iota((8, C), 0)
    nothing = jnp.zeros((8, C), F32)
    lefts = [pltpu.roll(x, 1, 1) for x in pairs]
    rights = [pltpu.roll(x, C - 1, 1) for x in pairs]
    for d in range(no):
        before = pairs[d - 1][:, C - 1 :] if d > 0 else jnp.zeros((8, 1), F32)
        after = pairs[d + 1][:, :1] if d < no - 1 else jnp.zeros((8, 1), F32)
        both = jnp.where(lane8 == row8, before, jnp.where(lane8 == row8 + 8, after, 0.0))
        edge_out[d] = jnp.sum(both, axis=0, keepdims=True)

        @pl.when(o != d)
        def _():
            ocn_copy(4, edge_out.at[d], edge_in.at[o], d).start()

    edge_in[o] = edge_out[o]

    def halo_copy(row, d, target):
        return pltpu.make_async_remote_copy(
            g.at[row, d], g_halo.at[1 - row], h_send.at[row], h_recv.at[1 - row],
            device_id=(target, d), device_id_type=MESH)

    @pl.when(first)
    def _():
        for d in range(no):
            halo_copy(0, d, a - 1).start()

    @pl.when(last)
    def _():
        for d in range(no):
            halo_copy(1, d, a + 1).start()

    wait_all(2, a2_in, 8 * (no - 1), False)

    @pl.when(has_above)
    def _():
        g_copy(0, g_up, 0, above).wait_recv()

    @pl.when(has_below)
    def _():
        g_copy(1, g_dn, 1, below).wait_recv()

    nt = (((1,), (1,)), ((), ()))
    for d in range(no):
        x = pairs[d]
        up = jnp.concatenate([g_up[d], x[:NSTATE]], axis=0)
        down = jnp.concatenate([x[NSTATE:], g_dn[d]], axis=0)
        left = jnp.where(lane8 == 0, lefts[d - 1] if d > 0 else nothing, lefts[d])
        right = jnp.where(lane8 == C - 1, rights[d + 1] if d < no - 1 else nothing, rights[d])
        wet8 = jnp.where(row8 < NSTATE, mask_in[d, 0:1], mask_in[d, 1:2])
        x = a2_in[8 * d : 8 * d + 8] + (x + tend(x, up + down + left + right - 4.0 * x, wet8, row8 % NSTATE))
        x = split(jnp.concatenate([x[:NSTATE], x[NSTATE:]], axis=1))
        f = lax.dot_general(x, whi[d], nt, preferred_element_type=F32) + lax.dot_general(
            x, wlo[d], nt, preferred_element_type=F32)
        f = f[:NSTATE] + f[NSTATE:]
        back[8 * d : 8 * d + 8] = jnp.concatenate([f[:, :C], f[:, C:]], axis=0)

    placed = jnp.dot(place, back[...], precision=HIGHEST, preferred_element_type=F32)
    for b in range(nb):
        ar[b] = placed[NSTATE * b : NSTATE * b + NSTATE]
    ar_copy = pltpu.make_async_copy(ar, ar_h, out_sem.at[0])
    ar_copy.start()

    wait_all(3, g_in, 8 * (no - 1), False)
    wait_all(4, edge_in, no - 1, False)

    @pl.when(has_up)
    def _():
        halo_copy(1, 0, a).wait_recv()

    @pl.when(has_dn)
    def _():
        halo_copy(0, 0, a).wait_recv()

    x = g_in[...]
    edge = jnp.concatenate([jnp.broadcast_to(edge_in[b], (8, C)) for b in range(no)], axis=0)
    lane, row = iota((r4, C), 1), iota((r4, C), 0)
    before = jnp.sum(jnp.where(lane == row % 8, edge, 0.0), axis=1, keepdims=True)
    after = jnp.sum(jnp.where(lane == row % 8 + 8, edge, 0.0), axis=1, keepdims=True)
    up = jnp.concatenate([g_halo[0], x[: r4 - NSTATE]], axis=0)
    down = jnp.concatenate([x[NSTATE:], g_halo[1]], axis=0)
    left = jnp.where(lane == 0, before, pltpu.roll(x, 1, 1))
    right = jnp.where(lane == C - 1, after, pltpu.roll(x, C - 1, 1))
    g_in[...] = a2_out[...] + (x + tend(x, up + down + left + right - 4.0 * x, wet, row % NSTATE))
    for s in range(NSTATE):
        on_t[s] = g_in[pl.ds(s, nb, stride=NSTATE), :]
    on_copy = pltpu.make_async_copy(on_t, on_h, out_sem.at[1])
    on_copy.start()

    wait_all(0, out1, nb - 1, True)
    wait_all(1, mask_out, no - 1, True)
    wait_all(2, a2_out, 8 * (no - 1), True)
    wait_all(3, gx, 8 * (no - 1), True)
    wait_all(4, edge_out, no - 1, True)
    for there, copy, _ in halos:
        @pl.when(there)
        def _():
            copy.wait_send()

    @pl.when(has_above)
    def _():
        g_copy(0, g_dn, 1, above).wait_send()

    @pl.when(has_below)
    def _():
        g_copy(1, g_up, 0, below).wait_send()

    for row, sends in ((0, first), (1, last)):
        @pl.when(sends)
        def _():
            pltpu.make_async_remote_copy(
                g.at[row], g_up, h_send.at[row], h_recv.at[1 - row], device_id=(a, o), device_id_type=MESH).wait_send()

    ar_copy.wait()
    on_copy.wait()


def body(na, no, atm_fields, coupler_map, remap_pattern, remap_weights, bulk_coeffs, ocean_state, land_mask):
    nb = atm_fields.shape[0]
    r4 = NSTATE * nb
    any_space = pl.BlockSpec(memory_space=pl.ANY)
    dma = pltpu.SemaphoreType.DMA
    return pl.pallas_call(
        functools.partial(kernel, na, no),
        out_shape=(
            jax.ShapeDtypeStruct(ocean_state.shape, F32),
            jax.ShapeDtypeStruct((nb, NSTATE, C), F32),
        ),
        in_specs=[any_space] * 7,
        out_specs=(any_space, any_space),
        scratch_shapes=[
            pltpu.VMEM((1, na * nb), jnp.int32),
            pltpu.SMEM((1, na * nb), jnp.int32),
            pltpu.SMEM((nb,), jnp.int32),
            pltpu.VMEM((NSTATE, F), F32),
            pltpu.VMEM((nb * F, C), F32),
            pltpu.VMEM((no, 2 * C, 2 * C), F32),
            pltpu.VMEM((no, 2 * C, 2 * C), BF16),
            pltpu.VMEM((no, 2 * C, 2 * C), BF16),
            pltpu.VMEM((NSTATE, nb, C), F32),
            pltpu.VMEM((nb, C), jnp.int32),
            pltpu.VMEM((nb, NSTATE, C), F32),
            pltpu.VMEM((nb, NSTATE, C), F32),
            pltpu.SMEM((nb,), jnp.int32),
            pltpu.VMEM((2, 3, NSTATE, C), F32),
            pltpu.VMEM((2, 3, NSTATE, C), F32),
            pltpu.VMEM((2, 4, r4), F32),
            pltpu.VMEM((6, 4, r4), F32),
            pltpu.VMEM((no, 2, C), F32),
            pltpu.VMEM((no, 2, C), F32),
            pltpu.VMEM((r4, C), F32),
            pltpu.VMEM((r4, C), F32),
            pltpu.VMEM((2, no, NSTATE, C), F32),
            pltpu.VMEM((no, NSTATE, C), F32),
            pltpu.VMEM((no, NSTATE, C), F32),
            pltpu.VMEM((r4, C), F32),
            pltpu.VMEM((r4, C), F32),
            pltpu.VMEM((no, 1, C), F32),
            pltpu.VMEM((no, 1, C), F32),
            pltpu.VMEM((2, NSTATE, C), F32),
            pltpu.VMEM((NSTATE, nb, C), F32),
            pltpu.VMEM((r4, C), F32),
            pltpu.VMEM((nb, NSTATE, C), F32),
            dma((7,)),
            dma((no,)),
            dma((5,)),
            dma((5,)),
            dma((2,)),
            dma((2,)),
            dma((6,)),
            dma((6,)),
            dma((2,)),
            dma((2,)),
            dma((2,)),
            dma((2,)),
            dma((2,)),
        ],
        compiler_params=pltpu.CompilerParams(
            collective_id=0, has_side_effects=True, vmem_limit_bytes=63 * 1024 * 1024
        ),
    )(
        atm_fields.reshape(nb * F, C),
        remap_weights.reshape(no, 2 * C, 2 * C),
        ocean_state,
        land_mask,
        coupler_map,
        remap_pattern,
        bulk_coeffs,
    )


def solution(mesh):
    in_specs = (
        P(("atm", "ocn"), None, None),
        P("ocn", None),
        P(("atm", "ocn")),
        P(("atm", "ocn"), None, None),
        P(),
        P(None, "atm", "ocn"),
        P("atm", "ocn"),
    )
    out_specs = (P(None, "atm", "ocn"), P(("atm", "ocn"), None, None))
    step = functools.partial(body, mesh.shape["atm"], mesh.shape["ocn"])
    return jax.shard_map(step, mesh=mesh, in_specs=in_specs, out_specs=out_specs, check_vma=False)
```

time: 62.8 us -> 53.6 us (0.85)
  the two profiles are of different devices: /device:TPU:1 before, /device:TPU:32 now
where the time goes in v2:
time: 53.6 us; the launch traced here: 53.3 us
  Pallas kernels  49.8 us (93%)
  local copies, waits for them, and re-layouts  2.95 us (6%)
  between operations  0.64 us (1%)
    pallas_call x1, Pallas kernels, body(): pl.pallas_call(functools.partial(kernel, na, no), out_shape=(jax.ShapeDty...  49.8 us
    unnamed x2, local copies, waits for them, and re-layouts  2.95 us

profile of v2, /device:TPU:32, one launch (start us, length us, event | category | flops | bytes accessed | tf_op | source)
XLA Modules:
  0.0 53.3 jit_solution(12279607425164188181)
XLA Ops:
  0.6 49.8 %shard_map.86 = (f32[4,32,128]{2,1,0:T(8,128)}, f32[32,4,128]{2,1,0:T(4,128)}) custom-call(f32[512,128]{1,0:T(8,128)} %bitcast.3, f32[16,256,256]{2,1,0:T(8,128)} %bitcast.2, f32[4,32,128]{2,1,0:T(8,128)} %st_h.1, s32[32,128]{1,0:T(8,128)} %mk_h.1, s32[1,1024]{1,0:T(1,128)} %cm_h.1, s32[32]{0:T(128)} %pat_h.1, f32[4,16]{1,0:T(4,128)} %c_h.1), custom_call_target="tpu_custom_call" | custom-call | tf_op jit(solution)/shard_map/pallas_call | solution.py:457
  50.4 1.5 %copy.11 = f32[4,32,128]{2,1,0:T(8,128)} copy(f32[4,32,128]{2,1,0:T(8,128)} %get-tuple-element.4) | data formatting | bytes 131072
  51.9 1.5 %copy.12 = f32[32,4,128]{2,1,0:T(4,128)} copy(f32[32,4,128]{2,1,0:T(4,128)} %get-tuple-element.5) | data formatting | bytes 131072

commit v3 on v2

--- a/solution.py
+++ b/solution.py
@@ -39,14 +39,14 @@
 def kernel(
     na, no,
     atm_h, w_h, st_h, mk_h, cm_h, pat_h, c_h,
-    on_h, ar_h,
+    flat, back,
     cm_v, cm_s, pat_s, c_v,
     atm, w32, whi, wlo, st, mk,
     out1, arr1, idx_s,
     row_out, row_in, col_out, col_in,
-    mask_out, mask_in, a2_out, a2_in,
-    g, g_up, g_dn, gx, g_in, edge_out, edge_in, g_halo, on_t, back, ar,
-    in_sem, w_sem, x_send, x_recv, row_send, row_recv, col_send, col_recv, g_send, g_recv, h_send, h_recv, out_sem,
+    mask_out, mask_in, a2_out, a2_in, a2_part, fix_out, fix_in,
+    g, g_up, g_dn, gx, g_in, edge_out, edge_in, g_halo,
+    in_sem, w_sem, x_send, x_recv, row_send, row_recv, col_send, col_recv, g_send, g_recv, h_send, h_recv,
 ):
     nb = na
     r4 = NSTATE * nb
@@ -216,6 +216,16 @@
     def rows_of(d):
         return pl.ds(pl.multiple_of(8 * d, 8), 8)
 
+    def alone(x):
+        lane, state = iota((r4, C), 1), iota((r4, C), 0) % NSTATE
+        none = jnp.zeros((NSTATE, C), F32)
+        up = jnp.concatenate([none, x[: r4 - NSTATE]], axis=0)
+        down = jnp.concatenate([x[NSTATE:], none], axis=0)
+        left = jnp.where(lane == 0, 0.0, pltpu.roll(x, 1, 1))
+        right = jnp.where(lane == C - 1, 0.0, pltpu.roll(x, C - 1, 1))
+        return tend(x, up + down + left + right - 4.0 * x, wet, state)
+
+    a2_part[...] = alone(alone(tile))
     pl.semaphore_wait(barrier, greetings)
     each(na, atm_peer, a, lambda to: block_copy(to).start())
     for there, copy, _ in halos:
@@ -239,13 +249,16 @@
         return carry
 
     lax.fori_loop(0, no, split_weights, 0)
-    across = iota((r4, r4), 1)
-    along = iota((r4, r4), 0)
-    pattern = jnp.zeros((1, r4), jnp.int32)
-    for r in range(nb):
-        pattern = jnp.where(iota((1, r4), 1) // NSTATE == r, pat_s[r], pattern)
-    place = jnp.logical_and(pattern == along // NSTATE, across % NSTATE == along % NSTATE)
-    place = jnp.where(place, 1.0, 0.0).astype(F32)
+
+    def a2_copy(src, to):
+        return ocn_copy(2, src.at[rows_of(to)], a2_in.at[rows_of(o)], to)
+
+    def send_inner(to):
+        @pl.when(jnp.logical_and(to > 0, to < no - 1))
+        def _():
+            a2_copy(a2_part, to).start()
+
+    each(no, ocn_peer, o, send_inner)
 
     for there, _, copy in halos:
         @pl.when(there)
@@ -289,7 +302,32 @@
     x = tend(x, rises(x) + of_x - 4.0 * x, wet_x, state)
     a2_out[...] = x[2 * NSTATE : 2 * NSTATE + r4]
     a2_in[rows_of(o)] = a2_out[rows_of(o)]
-    each(no, ocn_peer, o, lambda to: ocn_copy(2, a2_out.at[rows_of(to)], a2_in.at[rows_of(o)], to).start())
+    for to in (0, no - 1):
+        @pl.when(o != to)
+        def _():
+            a2_copy(a2_out, to).start()
+
+    def by_pair(columns):
+        lane, row = iota((r4, C), 1), iota((r4, C), 0) % 8
+        found = jnp.zeros((r4, C), F32)
+        for k, column in enumerate(columns):
+            found = jnp.where(lane == row + 8 * k, column, found)
+        return jnp.sum(found.reshape(no, 8, C), axis=1)
+
+    def by_row(packed, k):
+        lane, row = iota((r4, C), 1), iota((r4, C), 0) % 8
+        return jnp.sum(jnp.where(lane == row + 8 * k, packed, 0.0), axis=1, keepdims=True)
+
+    def spread(ref):
+        return jnp.concatenate([jnp.broadcast_to(ref[d], (8, C)) for d in range(no)], axis=0)
+
+    touched = (0, 1, C - 2, C - 1)
+    added = a2_out[...] - a2_part[...]
+    fix = by_pair([added[:, c : c + 1] for c in touched])
+    for d in range(no):
+        fix_out[d] = jnp.zeros((1, C), F32) if d in (0, no - 1) else fix[d : d + 1]
+    fix_in[o] = jnp.zeros((1, C), F32)
+    each(no, ocn_peer, o, lambda to: ocn_copy(5, fix_out.at[to], fix_in.at[o], to).start())
 
     def wait_all(i, ref, count, send):
         part = ref.at[pl.ds(0, count)]
@@ -313,11 +351,6 @@
         pairs.append(jnp.concatenate([upper, lower], axis=0))
         gx[8 * d : 8 * d + 8] = pairs[d]
 
-        @pl.when(o != d)
-        def _():
-            ocn_copy(3, gx.at[pl.ds(8 * d, 8)], g_in.at[rows_of(o)], d).start()
-
-    g_in[rows_of(o)] = gx[rows_of(o)]
     above = ((line - 1) // no, (line - 1) % no)
     below = ((line + 1) // no, (line + 1) % no)
 
@@ -325,6 +358,11 @@
         return pltpu.make_async_remote_copy(
             g.at[row], dst, g_send.at[row], g_recv.at[place], device_id=target, device_id_type=MESH)
 
+    def halo_copy(row, d, target):
+        return pltpu.make_async_remote_copy(
+            g.at[row, d], g_halo.at[1 - row], h_send.at[row], h_recv.at[1 - row],
+            device_id=(target, d), device_id_type=MESH)
+
     @pl.when(has_above)
     def _():
         g_copy(0, g_dn, 1, above).start()
@@ -333,38 +371,40 @@
     def _():
         g_copy(1, g_up, 0, below).start()
 
+    @pl.when(first)
+    def _():
+        for d in range(no):
+            halo_copy(0, d, a - 1).start()
+
+    @pl.when(last)
+    def _():
+        for d in range(no):
+            halo_copy(1, d, a + 1).start()
+
+    each(no, ocn_peer, o, lambda to: ocn_copy(3, gx.at[rows_of(to)], g_in.at[rows_of(o)], to).start())
+    g_in[rows_of(o)] = gx[rows_of(o)]
+
+    whole = gx[...]
+    one = jnp.zeros((8, 1), F32)
+    edge = by_pair([
+        jnp.concatenate([one, whole[: r4 - 8, C - 1 :]], axis=0),
+        jnp.concatenate([whole[8:, :1], one], axis=0)])
+    for d in range(no):
+        edge_out[d] = edge[d : d + 1]
+    each(no, ocn_peer, o, lambda to: ocn_copy(4, edge_out.at[to], edge_in.at[o], to).start())
+    edge_in[o] = edge_out[o]
     lane8, row8 = iota((8, C), 1), iota((8, C), 0)
     nothing = jnp.zeros((8, C), F32)
     lefts = [pltpu.roll(x, 1, 1) for x in pairs]
     rights = [pltpu.roll(x, C - 1, 1) for x in pairs]
-    for d in range(no):
-        before = pairs[d - 1][:, C - 1 :] if d > 0 else jnp.zeros((8, 1), F32)
-        after = pairs[d + 1][:, :1] if d < no - 1 else jnp.zeros((8, 1), F32)
-        both = jnp.where(lane8 == row8, before, jnp.where(lane8 == row8 + 8, after, 0.0))
-        edge_out[d] = jnp.sum(both, axis=0, keepdims=True)
-
-        @pl.when(o != d)
-        def _():
-            ocn_copy(4, edge_out.at[d], edge_in.at[o], d).start()
-
-    edge_in[o] = edge_out[o]
-
-    def halo_copy(row, d, target):
-        return pltpu.make_async_remote_copy(
-            g.at[row, d], g_halo.at[1 - row], h_send.at[row], h_recv.at[1 - row],
-            device_id=(target, d), device_id_type=MESH)
-
-    @pl.when(first)
-    def _():
-        for d in range(no):
-            halo_copy(0, d, a - 1).start()
-
-    @pl.when(last)
-    def _():
-        for d in range(no):
-            halo_copy(1, d, a + 1).start()
 
     wait_all(2, a2_in, 8 * (no - 1), False)
+    wait_all(5, fix_in, no - 1, False)
+    packed = spread(fix_in)
+    x = a2_in[...]
+    for k, c in enumerate(touched):
+        x = x + jnp.where(iota((r4, C), 1) == c, by_row(packed, k), 0.0)
+    a2_in[...] = x
 
     @pl.when(has_above)
     def _():
@@ -389,12 +429,6 @@
         f = f[:NSTATE] + f[NSTATE:]
         back[8 * d : 8 * d + 8] = jnp.concatenate([f[:, :C], f[:, C:]], axis=0)
 
-    placed = jnp.dot(place, back[...], precision=HIGHEST, preferred_element_type=F32)
-    for b in range(nb):
-        ar[b] = placed[NSTATE * b : NSTATE * b + NSTATE]
-    ar_copy = pltpu.make_async_copy(ar, ar_h, out_sem.at[0])
-    ar_copy.start()
-
     wait_all(3, g_in, 8 * (no - 1), False)
     wait_all(4, edge_in, no - 1, False)
 
@@ -407,25 +441,21 @@
         halo_copy(0, 0, a).wait_recv()
 
     x = g_in[...]
-    edge = jnp.concatenate([jnp.broadcast_to(edge_in[b], (8, C)) for b in range(no)], axis=0)
+    edge = spread(edge_in)
     lane, row = iota((r4, C), 1), iota((r4, C), 0)
-    before = jnp.sum(jnp.where(lane == row % 8, edge, 0.0), axis=1, keepdims=True)
-    after = jnp.sum(jnp.where(lane == row % 8 + 8, edge, 0.0), axis=1, keepdims=True)
+    before, after = by_row(edge, 0), by_row(edge, 1)
     up = jnp.concatenate([g_halo[0], x[: r4 - NSTATE]], axis=0)
     down = jnp.concatenate([x[NSTATE:], g_halo[1]], axis=0)
     left = jnp.where(lane == 0, before, pltpu.roll(x, 1, 1))
     right = jnp.where(lane == C - 1, after, pltpu.roll(x, C - 1, 1))
-    g_in[...] = a2_out[...] + (x + tend(x, up + down + left + right - 4.0 * x, wet, row % NSTATE))
-    for s in range(NSTATE):
-        on_t[s] = g_in[pl.ds(s, nb, stride=NSTATE), :]
-    on_copy = pltpu.make_async_copy(on_t, on_h, out_sem.at[1])
-    on_copy.start()
+    flat[...] = a2_out[...] + (x + tend(x, up + down + left + right - 4.0 * x, wet, row % NSTATE))
 
     wait_all(0, out1, nb - 1, True)
     wait_all(1, mask_out, no - 1, True)
     wait_all(2, a2_out, 8 * (no - 1), True)
     wait_all(3, gx, 8 * (no - 1), True)
     wait_all(4, edge_out, no - 1, True)
+    wait_all(5, fix_out, no - 1, True)
     for there, copy, _ in halos:
         @pl.when(there)
         def _():
@@ -445,23 +475,25 @@
             pltpu.make_async_remote_copy(
                 g.at[row], g_up, h_send.at[row], h_recv.at[1 - row], device_id=(a, o), device_id_type=MESH).wait_send()
 
-    ar_copy.wait()
-    on_copy.wait()
+
+def finish(nb, pat_s, flat, back, on, returned):
+    for s in range(NSTATE):
+        on[s] = flat[pl.ds(s, nb, stride=NSTATE), :]
+    for r in range(nb):
+        returned[pat_s[r]] = back[NSTATE * r : NSTATE * r + NSTATE]
 
 
 def body(na, no, atm_fields, coupler_map, remap_pattern, remap_weights, bulk_coeffs, ocean_state, land_mask):
     nb = atm_fields.shape[0]
     r4 = NSTATE * nb
     any_space = pl.BlockSpec(memory_space=pl.ANY)
+    vmem = pl.BlockSpec(memory_space=pltpu.VMEM)
     dma = pltpu.SemaphoreType.DMA
-    return pl.pallas_call(
+    flat, back = pl.pallas_call(
         functools.partial(kernel, na, no),
-        out_shape=(
-            jax.ShapeDtypeStruct(ocean_state.shape, F32),
-            jax.ShapeDtypeStruct((nb, NSTATE, C), F32),
-        ),
+        out_shape=(pltpu.VMEM((r4, C), F32), pltpu.VMEM((r4, C), F32)),
         in_specs=[any_space] * 7,
-        out_specs=(any_space, any_space),
+        out_specs=(vmem, vmem),
         scratch_shapes=[
             pltpu.VMEM((1, na * nb), jnp.int32),
             pltpu.SMEM((1, na * nb), jnp.int32),
@@ -484,6 +516,9 @@
             pltpu.VMEM((no, 2, C), F32),
             pltpu.VMEM((r4, C), F32),
             pltpu.VMEM((r4, C), F32),
+            pltpu.VMEM((r4, C), F32),
+            pltpu.VMEM((no, 1, C), F32),
+            pltpu.VMEM((no, 1, C), F32),
             pltpu.VMEM((2, no, NSTATE, C), F32),
             pltpu.VMEM((no, NSTATE, C), F32),
             pltpu.VMEM((no, NSTATE, C), F32),
@@ -492,13 +527,10 @@
             pltpu.VMEM((no, 1, C), F32),
             pltpu.VMEM((no, 1, C), F32),
             pltpu.VMEM((2, NSTATE, C), F32),
-            pltpu.VMEM((NSTATE, nb, C), F32),
-            pltpu.VMEM((r4, C), F32),
-            pltpu.VMEM((nb, NSTATE, C), F32),
             dma((7,)),
             dma((no,)),
-            dma((5,)),
-            dma((5,)),
+            dma((6,)),
+            dma((6,)),
             dma((2,)),
             dma((2,)),
             dma((6,)),
@@ -507,10 +539,9 @@
             dma((2,)),
             dma((2,)),
             dma((2,)),
-            dma((2,)),
         ],
         compiler_params=pltpu.CompilerParams(
-            collective_id=0, has_side_effects=True, vmem_limit_bytes=63 * 1024 * 1024
+            collective_id=0, has_side_effects=True, vmem_limit_bytes=60 * 1024 * 1024
         ),
     )(
         atm_fields.reshape(nb * F, C),
@@ -521,6 +552,16 @@
         remap_pattern,
         bulk_coeffs,
     )
+    return pl.pallas_call(
+        functools.partial(finish, nb),
+        out_shape=(
+            jax.ShapeDtypeStruct(ocean_state.shape, F32),
+            jax.ShapeDtypeStruct((nb, NSTATE, C), F32),
+        ),
+        in_specs=[pl.BlockSpec(memory_space=pltpu.SMEM), vmem, vmem],
+        out_specs=(vmem, vmem),
+        compiler_params=pltpu.CompilerParams(vmem_limit_bytes=4 * 1024 * 1024),
+    )(remap_pattern, flat, back)
 
 
 def solution(mesh):

time: 53.6 us -> 47.7 us (0.89)
  the two profiles are of different devices: /device:TPU:32 before, /device:TPU:57 now
where the time goes in v3:
time: 47.7 us; the launch traced here: 47.6 us
  Pallas kernels  46.9 us (98%)
  between operations  0.66 us (1%)
    pallas_call x1, Pallas kernels, body(): pl.pallas_call(functools.partial(kernel, na, no), out_shape=(pltpu.VMEM((...  45.7 us
    pallas_call x1, Pallas kernels, body(): pl.pallas_call(functools.partial(finish, nb), out_shape=(jax.ShapeDtypeSt...  1.22 us

profile of v3, /device:TPU:57, one launch (start us, length us, event | category | flops | bytes accessed | tf_op | source)
XLA Modules:
  0.0 47.6 jit_solution(14684467807786189446)
XLA Ops:
  0.6 0.0 copy-start
  0.6 45.7 %shard_map.86 = (f32[128,128]{1,0:T(8,128)S(1)}, f32[128,128]{1,0:T(8,128)S(1)}) custom-call(f32[512,128]{1,0:T(8,128)} %bitcast.3, f32[16,256,256]{2,1,0:T(8,128)} %bitcast.2, f32[4,32,128]{2,1,0:T(8,128)} %st_h.1, s32[32,128]{1,0:T(8,128)} %mk_h.1, s32[1,1024]{1,0:T(1,128)} %cm_h.1, s32[32]{0:T(128)} %pat_s.1, f32[4,16]{1,0:T(4,128)} %c_h.1), custom_call_target="tpu_custom_call" | custom-call | tf_op jit(solution)/shard_map/pallas_call | solution.py:492
  46.3 0.0 copy-done
  46.3 1.2 %shard_map.87 = (f32[4,32,128]{2,1,0:T(8,128)}, f32[32,4,128]{2,1,0:T(4,128)}) custom-call(s32[32]{0:T(128)S(1)} %copy-done, f32[128,128]{1,0:T(8,128)S(1)} %get-tuple-element.4.flat, f32[128,128]{1,0:T(8,128)S(1)} %get-tuple-element.5.back), custom_call_target="tpu_custom_call" | custom-call | tf_op jit(solution)/shard_map/pallas_call | solution.py:555
Async XLA Ops:
  0.6 45.7 %copy-start = (s32[32]{0:T(128)S(1)}, s32[32]{0:T(128)}, u32[]{:S(2)}) copy-start(s32[32]{0:T(128)} %pat_s.1) | copy-start | bytes 388

commit v4 on v3

--- a/solution.py
+++ b/solution.py
@@ -39,13 +39,13 @@
 def kernel(
     na, no,
     atm_h, w_h, st_h, mk_h, cm_h, pat_h, c_h,
-    flat, back,
+    on, returned,
     cm_v, cm_s, pat_s, c_v,
     atm, w32, whi, wlo, st, mk,
     out1, arr1, idx_s,
     row_out, row_in, col_out, col_in,
     mask_out, mask_in, a2_out, a2_in, a2_part, fix_out, fix_in,
-    g, g_up, g_dn, gx, g_in, edge_out, edge_in, g_halo,
+    g, g_up, g_dn, gx, g_in, edge_out, edge_in, g_halo, back,
     in_sem, w_sem, x_send, x_recv, row_send, row_recv, col_send, col_recv, g_send, g_recv, h_send, h_recv,
 ):
     nb = na
@@ -54,39 +54,29 @@
     o = lax.axis_index("ocn")
     line = a * no + o
 
-    nz = na // 4
-    half = (a // 4) // (nz // 2)
-    nx = no // 4
-
-    def atm_peer(k):
-        i = k // 4
-        return (i * half + (nz - 1 - i) * (1 - half)) * 4 + k % 4
-
-    def ocn_peer(k):
-        rest = k % (no // 2)
-        x = (o // 4 + rest // 2 + nx // 2) % nx
-        z = (o // 2 + 1 + k // (no // 2)) % 2
-        return x * 4 + z * 2 + (o + rest) % 2
-
-    def each(count, peer, me, act):
-        def step(k, carry):
-            to = peer(k)
-
-            @pl.when(to != me)
-            def _():
-                act(to)
-
-            return carry
-
-        lax.fori_loop(0, count, step, 0)
+    nz, nx = na // 4, no // 4
+    zs = [lax.rem(lax.div(a, 4) + k, nz) * 4 for k in range(nz)]
+    ys = [lax.rem(lax.rem(a, 4) + k, 4) for k in range(4)]
+    xs = [lax.rem(lax.div(o, 4) + k, nx) * 4 for k in range(nx)]
+    hs = [lax.rem(lax.div(o, 2) + k, 2) * 2 for k in range(2)]
+    cs = [lax.rem(o + k, 2) for k in range(2)]
+    z_order = [k for i in range(1, nz // 2 + 1) for k in ((nz - i, i) if nz - i != i else (i,))]
+    atm_far = [zs[k] + ys[y] for k in z_order for y in (2, 1, 3, 0)]
+    atm_near = [zs[0] + ys[y] for y in (2, 1, 3)]
+    x_order = [nx // 2] + [k for k in range(nx) if k != nx // 2]
+    ocn_far = [xs[k] + hs[1] + cs[c] for k in x_order for c in (1, 0)]
+    ocn_near = [xs[k] + hs[0] + cs[c] for k in x_order for c in (1, 0) if k or c]
+    atm_peers, ocn_peers = atm_far + atm_near, ocn_far + ocn_near
 
     barrier = pltpu.get_barrier_semaphore()
 
     def greet(device):
         pl.semaphore_signal(barrier, inc=1, device_id=device, device_id_type=MESH)
 
-    each(no, ocn_peer, o, lambda to: greet((a, to)))
-    each(na, atm_peer, a, lambda to: greet((to, o)))
+    for to in ocn_far:
+        greet((a, to))
+    for to in atm_far:
+        greet((to, o))
     has_up, has_dn, has_left, has_right = a > 0, a < na - 1, o > 0, o < no - 1
     corners = []
     for dv, vert in ((-1, has_up), (1, has_dn)):
@@ -101,6 +91,10 @@
             def _():
                 greet((a + dv, o + dh))
 
+    for to in ocn_near:
+        greet((a, to))
+    for to in atm_near:
+        greet((to, o))
     first = jnp.logical_and(o == 0, has_up)
     last = jnp.logical_and(o == no - 1, has_dn)
     greetings = na + no - 2 + no * (first.astype(jnp.int32) + last.astype(jnp.int32))
@@ -227,13 +221,18 @@
 
     a2_part[...] = alone(alone(tile))
     pl.semaphore_wait(barrier, greetings)
-    each(na, atm_peer, a, lambda to: block_copy(to).start())
+    for to in atm_far[: na // 2]:
+        block_copy(to).start()
+    for to in ocn_far:
+        ocn_copy(1, mask_out.at[to], mask_in.at[o], to).start()
+    for to in atm_far[na // 2 :] + atm_near:
+        block_copy(to).start()
+    for to in ocn_near:
+        ocn_copy(1, mask_out.at[to], mask_in.at[o], to).start()
     for there, copy, _ in halos:
         @pl.when(there)
         def _():
             copy.start()
-
-    each(no, ocn_peer, o, lambda to: ocn_copy(1, mask_out.at[to], mask_in.at[o], to).start())
 
     copies[5].wait()
     copies[6].wait()
@@ -250,6 +249,14 @@
 
     lax.fori_loop(0, no, split_weights, 0)
 
+    across = iota((r4, r4), 1)
+    along = iota((r4, r4), 0)
+    pattern = jnp.zeros((1, r4), jnp.int32)
+    for r in range(nb):
+        pattern = jnp.where(iota((1, r4), 1) // NSTATE == r, pat_s[r], pattern)
+    place = jnp.logical_and(pattern == along // NSTATE, across % NSTATE == along % NSTATE)
+    place = jnp.where(place, 1.0, 0.0).astype(F32)
+
     def a2_copy(src, to):
         return ocn_copy(2, src.at[rows_of(to)], a2_in.at[rows_of(o)], to)
 
@@ -258,7 +265,8 @@
         def _():
             a2_copy(a2_part, to).start()
 
-    each(no, ocn_peer, o, send_inner)
+    for to in ocn_peers:
+        send_inner(to)
 
     for there, _, copy in halos:
         @pl.when(there)
@@ -327,7 +335,8 @@
     for d in range(no):
         fix_out[d] = jnp.zeros((1, C), F32) if d in (0, no - 1) else fix[d : d + 1]
     fix_in[o] = jnp.zeros((1, C), F32)
-    each(no, ocn_peer, o, lambda to: ocn_copy(5, fix_out.at[to], fix_in.at[o], to).start())
+    for to in ocn_peers:
+        ocn_copy(5, fix_out.at[to], fix_in.at[o], to).start()
 
     def wait_all(i, ref, count, send):
         part = ref.at[pl.ds(0, count)]
@@ -381,7 +390,8 @@
         for d in range(no):
             halo_copy(1, d, a + 1).start()
 
-    each(no, ocn_peer, o, lambda to: ocn_copy(3, gx.at[rows_of(to)], g_in.at[rows_of(o)], to).start())
+    for to in ocn_peers:
+        ocn_copy(3, gx.at[rows_of(to)], g_in.at[rows_of(o)], to).start()
     g_in[rows_of(o)] = gx[rows_of(o)]
 
     whole = gx[...]
@@ -391,7 +401,8 @@
         jnp.concatenate([whole[8:, :1], one], axis=0)])
     for d in range(no):
         edge_out[d] = edge[d : d + 1]
-    each(no, ocn_peer, o, lambda to: ocn_copy(4, edge_out.at[to], edge_in.at[o], to).start())
+    for to in ocn_peers:
+        ocn_copy(4, edge_out.at[to], edge_in.at[o], to).start()
     edge_in[o] = edge_out[o]
     lane8, row8 = iota((8, C), 1), iota((8, C), 0)
     nothing = jnp.zeros((8, C), F32)
@@ -429,6 +440,10 @@
         f = f[:NSTATE] + f[NSTATE:]
         back[8 * d : 8 * d + 8] = jnp.concatenate([f[:, :C], f[:, C:]], axis=0)
 
+    placed = jnp.dot(place, back[...], precision=HIGHEST, preferred_element_type=F32)
+    for b in range(nb):
+        returned[b] = placed[NSTATE * b : NSTATE * b + NSTATE]
+
     wait_all(3, g_in, 8 * (no - 1), False)
     wait_all(4, edge_in, no - 1, False)
 
@@ -448,7 +463,9 @@
     down = jnp.concatenate([x[NSTATE:], g_halo[1]], axis=0)
     left = jnp.where(lane == 0, before, pltpu.roll(x, 1, 1))
     right = jnp.where(lane == C - 1, after, pltpu.roll(x, C - 1, 1))
-    flat[...] = a2_out[...] + (x + tend(x, up + down + left + right - 4.0 * x, wet, row % NSTATE))
+    back[...] = a2_out[...] + (x + tend(x, up + down + left + right - 4.0 * x, wet, row % NSTATE))
+    for s in range(NSTATE):
+        on[s] = back[pl.ds(s, nb, stride=NSTATE), :]
 
     wait_all(0, out1, nb - 1, True)
     wait_all(1, mask_out, no - 1, True)
@@ -476,11 +493,12 @@
                 g.at[row], g_up, h_send.at[row], h_recv.at[1 - row], device_id=(a, o), device_id_type=MESH).wait_send()
 
 
-def finish(nb, pat_s, flat, back, on, returned):
-    for s in range(NSTATE):
-        on[s] = flat[pl.ds(s, nb, stride=NSTATE), :]
-    for r in range(nb):
-        returned[pat_s[r]] = back[NSTATE * r : NSTATE * r + NSTATE]
+def finish(on, returned, on_h, returned_h, sems):
+    copies = [pltpu.make_async_copy(on, on_h, sems.at[0]), pltpu.make_async_copy(returned, returned_h, sems.at[1])]
+    for copy in copies:
+        copy.start()
+    for copy in copies:
+        copy.wait()
 
 
 def body(na, no, atm_fields, coupler_map, remap_pattern, remap_weights, bulk_coeffs, ocean_state, land_mask):
@@ -489,9 +507,9 @@
     any_space = pl.BlockSpec(memory_space=pl.ANY)
     vmem = pl.BlockSpec(memory_space=pltpu.VMEM)
     dma = pltpu.SemaphoreType.DMA
-    flat, back = pl.pallas_call(
+    on, returned = pl.pallas_call(
         functools.partial(kernel, na, no),
-        out_shape=(pltpu.VMEM((r4, C), F32), pltpu.VMEM((r4, C), F32)),
+        out_shape=(pltpu.VMEM((NSTATE, nb, C), F32), pltpu.VMEM((nb, NSTATE, C), F32)),
         in_specs=[any_space] * 7,
         out_specs=(vmem, vmem),
         scratch_shapes=[
@@ -527,6 +545,7 @@
             pltpu.VMEM((no, 1, C), F32),
             pltpu.VMEM((no, 1, C), F32),
             pltpu.VMEM((2, NSTATE, C), F32),
+            pltpu.VMEM((r4, C), F32),
             dma((7,)),
             dma((no,)),
             dma((6,)),
@@ -553,15 +572,16 @@
         bulk_coeffs,
     )
     return pl.pallas_call(
-        functools.partial(finish, nb),
+        finish,
         out_shape=(
             jax.ShapeDtypeStruct(ocean_state.shape, F32),
             jax.ShapeDtypeStruct((nb, NSTATE, C), F32),
         ),
-        in_specs=[pl.BlockSpec(memory_space=pltpu.SMEM), vmem, vmem],
-        out_specs=(vmem, vmem),
+        in_specs=[any_space, any_space],
+        out_specs=(any_space, any_space),
+        scratch_shapes=[dma((2,))],
         compiler_params=pltpu.CompilerParams(vmem_limit_bytes=4 * 1024 * 1024),
-    )(remap_pattern, flat, back)
+    )(on, returned)
 
 
 def solution(mesh):

time: 47.7 us -> 45.1 us (0.945)
  the two profiles are of different devices: /device:TPU:57 before, /device:TPU:1 now
where the time goes in v4:
time: 45.1 us; the launch traced here: 44.9 us
  Pallas kernels  44.3 us (98%)
  between operations  0.64 us (1%)
    pallas_call x1, Pallas kernels, body(): pl.pallas_call(functools.partial(kernel, na, no), out_shape=(pltpu.VMEM((...  43.6 us

profile of v4, /device:TPU:1, one launch (start us, length us, event | category | flops | bytes accessed | tf_op | source)
XLA Modules:
  0.0 44.9 jit_solution(12026821812454835903)
XLA Ops:
  0.6 43.6 %shard_map.86 = (f32[4,32,128]{2,1,0:T(8,128)S(1)}, f32[32,4,128]{2,1,0:T(4,128)S(1)}) custom-call(f32[512,128]{1,0:T(8,128)} %bitcast.3, f32[16,256,256]{2,1,0:T(8,128)} %bitcast.2, f32[4,32,128]{2,1,0:T(8,128)} %st_h.1, s32[32,128]{1,0:T(8,128)} %mk_h.1, s32[1,1024]{1,0:T(1,128)} %cm_h.1, s32[32]{0:T(128)} %pat_h.1, f32[4,16]{1,0:T(4,128)} %c_h.1), custom_call_target="tpu_custom_call" | custom-call | tf_op jit(solution)/shard_map/pallas_call | solution.py:510
  44.3 0.7 %shard_map.87 = (f32[4,32,128]{2,1,0:T(8,128)}, f32[32,4,128]{2,1,0:T(4,128)}) custom-call(f32[4,32,128]{2,1,0:T(8,128)S(1)} %get-tuple-element.4.on, f32[32,4,128]{2,1,0:T(4,128)S(1)} %get-tuple-element.5.returned), custom_call_target="tpu_custom_call" | custom-call | tf_op jit(solution)/shard_map/pallas_call | solution.py:574

commit v5 on v4

--- a/solution.py
+++ b/solution.py
@@ -255,7 +255,7 @@
     for r in range(nb):
         pattern = jnp.where(iota((1, r4), 1) // NSTATE == r, pat_s[r], pattern)
     place = jnp.logical_and(pattern == along // NSTATE, across % NSTATE == along % NSTATE)
-    place = jnp.where(place, 1.0, 0.0).astype(F32)
+    place = jnp.where(place, 1.0, 0.0).astype(BF16)
 
     def a2_copy(src, to):
         return ocn_copy(2, src.at[rows_of(to)], a2_in.at[rows_of(o)], to)
@@ -265,14 +265,14 @@
         def _():
             a2_copy(a2_part, to).start()
 
+
+    for there, _, copy in halos:
+        @pl.when(there)
+        def _():
+            copy.wait_recv()
+
     for to in ocn_peers:
         send_inner(to)
-
-    for there, _, copy in halos:
-        @pl.when(there)
-        def _():
-            copy.wait_recv()
-
     at, along_lane = iota((C, r4), 0), iota((C, r4), 1)
     beside = jnp.zeros((C, r4), F32)
     for i in range(3):
@@ -348,50 +348,58 @@
 
     wait_all(1, mask_in, no - 1, False)
     wait_all(0, arr1, nb - 1, False)
-    pairs = []
-    for d in range(no):
-        x = jnp.concatenate([arr1[idx_s[2 * d]], arr1[idx_s[2 * d + 1]]], axis=1)
-        x = split(x)
-        f = jnp.dot(x, whi[d], preferred_element_type=F32) + jnp.dot(x, wlo[d], preferred_element_type=F32)
-        f = 0.25 * (f[:NSTATE] + f[NSTATE:])
-        upper, lower = f[:, :C] * mask_in[d, 0:1], f[:, C:] * mask_in[d, 1:2]
-        g[0, d] = upper
-        g[1, d] = lower
-        pairs.append(jnp.concatenate([upper, lower], axis=0))
-        gx[8 * d : 8 * d + 8] = pairs[d]
-
     above = ((line - 1) // no, (line - 1) % no)
     below = ((line + 1) // no, (line + 1) % no)
 
-    def g_copy(row, dst, place, target):
+    def g_copy(row, dst, place, target, part=None):
+        src = g.at[row]
+        if part is not None:
+            src, dst = src.at[part], dst.at[part]
         return pltpu.make_async_remote_copy(
-            g.at[row], dst, g_send.at[row], g_recv.at[place], device_id=target, device_id_type=MESH)
+            src, dst, g_send.at[row], g_recv.at[place], device_id=target, device_id_type=MESH)
 
     def halo_copy(row, d, target):
         return pltpu.make_async_remote_copy(
             g.at[row, d], g_halo.at[1 - row], h_send.at[row], h_recv.at[1 - row],
             device_id=(target, d), device_id_type=MESH)
 
-    @pl.when(has_above)
-    def _():
-        g_copy(0, g_dn, 1, above).start()
-
-    @pl.when(has_below)
-    def _():
-        g_copy(1, g_up, 0, below).start()
-
-    @pl.when(first)
-    def _():
-        for d in range(no):
-            halo_copy(0, d, a - 1).start()
-
-    @pl.when(last)
-    def _():
-        for d in range(no):
-            halo_copy(1, d, a + 1).start()
-
-    for to in ocn_peers:
-        ocn_copy(3, gx.at[rows_of(to)], g_in.at[rows_of(o)], to).start()
+    pairs = []
+    for q in range(no // 4):
+        part = range(4 * q, 4 * q + 4)
+        for d in part:
+            x = split(jnp.concatenate([arr1[idx_s[2 * d]], arr1[idx_s[2 * d + 1]]], axis=1))
+            f = jnp.dot(x, whi[d], preferred_element_type=F32) + jnp.dot(x, wlo[d], preferred_element_type=F32)
+            f = 0.25 * (f[:NSTATE] + f[NSTATE:])
+            pairs.append(jnp.concatenate([f[:, :C] * mask_in[d, 0:1], f[:, C:] * mask_in[d, 1:2]], axis=0))
+        for d in part:
+            gx[8 * d : 8 * d + 8] = pairs[d]
+            g[0, d] = pairs[d][:NSTATE]
+            g[1, d] = pairs[d][NSTATE:]
+        here = pl.ds(4 * q, 4)
+
+        @pl.when(has_above)
+        def _():
+            g_copy(0, g_dn, 1, above, here).start()
+
+        @pl.when(has_below)
+        def _():
+            g_copy(1, g_up, 0, below, here).start()
+
+        @pl.when(first)
+        def _():
+            for d in part:
+                halo_copy(0, d, a - 1).start()
+
+        @pl.when(last)
+        def _():
+            for d in part:
+                halo_copy(1, d, a + 1).start()
+
+        for d in part:
+            @pl.when(o != d)
+            def _():
+                ocn_copy(3, gx.at[pl.ds(8 * d, 8)], g_in.at[rows_of(o)], d).start()
+
     g_in[rows_of(o)] = gx[rows_of(o)]
 
     whole = gx[...]
@@ -440,7 +448,13 @@
         f = f[:NSTATE] + f[NSTATE:]
         back[8 * d : 8 * d + 8] = jnp.concatenate([f[:, :C], f[:, C:]], axis=0)
 
-    placed = jnp.dot(place, back[...], precision=HIGHEST, preferred_element_type=F32)
+    x = back[...]
+    high = x.astype(BF16)
+    rest = x - high.astype(F32)
+    middle = rest.astype(BF16)
+    low = (rest - middle.astype(F32)).astype(BF16)
+    placed = jnp.dot(place, jnp.concatenate([high, middle, low], axis=1), preferred_element_type=F32)
+    placed = placed[:, :C] + placed[:, C : 2 * C] + placed[:, 2 * C :]
     for b in range(nb):
         returned[b] = placed[NSTATE * b : NSTATE * b + NSTATE]
 

time: 45.1 us -> 43.8 us (0.971)
  Pallas kernels: 44.3 us -> 43.1 us
    pallas_call x1, Pallas kernels: 43.6 us -> 42.4 us  [body(): pl.pallas_call(functools.partial(kernel, na, no), out_shape=(pltpu.VMEM((...]
where the time goes in v5:
time: 43.8 us; the launch traced here: 43.7 us
  Pallas kernels  43.1 us (98%)
  between operations  0.64 us (1%)
    pallas_call x1, Pallas kernels, body(): pl.pallas_call(functools.partial(kernel, na, no), out_shape=(pltpu.VMEM((...  42.4 us

profile of v5, /device:TPU:1, one launch (start us, length us, event | category | flops | bytes accessed | tf_op | source)
XLA Modules:
  0.0 43.7 jit_solution(3188790000982122398)
XLA Ops:
  0.6 42.4 %shard_map.86 = (f32[4,32,128]{2,1,0:T(8,128)S(1)}, f32[32,4,128]{2,1,0:T(4,128)S(1)}) custom-call(f32[512,128]{1,0:T(8,128)} %bitcast.3, f32[16,256,256]{2,1,0:T(8,128)} %bitcast.2, f32[4,32,128]{2,1,0:T(8,128)} %st_h.1, s32[32,128]{1,0:T(8,128)} %mk_h.1, s32[1,1024]{1,0:T(1,128)} %cm_h.1, s32[32]{0:T(128)} %pat_h.1, f32[4,16]{1,0:T(4,128)} %c_h.1), custom_call_target="tpu_custom_call" | custom-call | tf_op jit(solution)/shard_map/pallas_call | solution.py:524
  43.0 0.7 %shard_map.87 = (f32[4,32,128]{2,1,0:T(8,128)}, f32[32,4,128]{2,1,0:T(4,128)}) custom-call(f32[4,32,128]{2,1,0:T(8,128)S(1)} %get-tuple-element.4.on, f32[32,4,128]{2,1,0:T(4,128)S(1)} %get-tuple-element.5.returned), custom_call_target="tpu_custom_call" | custom-call | tf_op jit(solution)/shard_map/pallas_call | solution.py:588

commit v6 on v5

--- a/solution.py
+++ b/solution.py
@@ -266,12 +266,15 @@
             a2_copy(a2_part, to).start()
 
 
+    for to in ocn_near:
+        send_inner(to)
+
     for there, _, copy in halos:
         @pl.when(there)
         def _():
             copy.wait_recv()
 
-    for to in ocn_peers:
+    for to in ocn_far:
         send_inner(to)
     at, along_lane = iota((C, r4), 0), iota((C, r4), 1)
     beside = jnp.zeros((C, r4), F32)
@@ -395,10 +398,13 @@
             for d in part:
                 halo_copy(1, d, a + 1).start()
 
-        for d in part:
-            @pl.when(o != d)
-            def _():
-                ocn_copy(3, gx.at[pl.ds(8 * d, 8)], g_in.at[rows_of(o)], d).start()
+        for apart in (True, False):
+            for d in part:
+                far = lax.rem(lax.div(o, 2), 2) != d // 2 % 2
+
+                @pl.when(far if apart else jnp.logical_and(jnp.logical_not(far), o != d))
+                def _():
+                    ocn_copy(3, gx.at[pl.ds(8 * d, 8)], g_in.at[rows_of(o)], d).start()
 
     g_in[rows_of(o)] = gx[rows_of(o)]
 

time: 43.8 us -> 43.8 us (level)
  no operation moved by 1% of the time
where the time goes in v6:
time: 43.8 us; the launch traced here: 43.7 us
  Pallas kernels  43.1 us (98%)
  between operations  0.64 us (1%)
    pallas_call x1, Pallas kernels, body(): pl.pallas_call(functools.partial(kernel, na, no), out_shape=(pltpu.VMEM((...  42.4 us

profile of v6, /device:TPU:1, one launch (start us, length us, event | category | flops | bytes accessed | tf_op | source)
XLA Modules:
  0.0 43.7 jit_solution(8909775327226099667)
XLA Ops:
  0.6 42.4 %shard_map.86 = (f32[4,32,128]{2,1,0:T(8,128)S(1)}, f32[32,4,128]{2,1,0:T(4,128)S(1)}) custom-call(f32[512,128]{1,0:T(8,128)} %bitcast.3, f32[16,256,256]{2,1,0:T(8,128)} %bitcast.2, f32[4,32,128]{2,1,0:T(8,128)} %st_h.1, s32[32,128]{1,0:T(8,128)} %mk_h.1, s32[1,1024]{1,0:T(1,128)} %cm_h.1, s32[32]{0:T(128)} %pat_h.1, f32[4,16]{1,0:T(4,128)} %c_h.1), custom_call_target="tpu_custom_call" | custom-call | tf_op jit(solution)/shard_map/pallas_call | solution.py:530
  43.0 0.7 %shard_map.87 = (f32[4,32,128]{2,1,0:T(8,128)}, f32[32,4,128]{2,1,0:T(4,128)}) custom-call(f32[4,32,128]{2,1,0:T(8,128)S(1)} %get-tuple-element.4.on, f32[32,4,128]{2,1,0:T(4,128)S(1)} %get-tuple-element.5.returned), custom_call_target="tpu_custom_call" | custom-call | tf_op jit(solution)/shard_map/pallas_call | solution.py:594
